TPU v7x, 32 devices: a whole 2x2x4 slice. The times are simulated.
32 devices in a mesh: tok: 16 (over z, x, core), head: 2 (over y).
Axes of the slice: x: 2, y: 2, z: 4, core: 2. Of those that a mesh axis runs over, the one named last changes fastest.
Arguments:
- qkv: bfloat16 [3, 4096, 768], P(None, 'tok', 'head'), may hold values from -8 to 8
- token_rank: int32 [12, 4096], P('head', 'tok'), may hold values from 0 to 4095, as said below
- cluster_sizes: int32 [12, 64], P('head'), may hold values from 1 to 477, as said below
- cluster_owner: int32 [12, 64], P('head'), may hold values from 0 to 15, as said below
- cache_zero: bfloat16 [4096, 768], P('tok', 'head'), may hold values from -1.796875 to 1.796875
- cache_one: bfloat16 [4096, 768], P('tok', 'head'), may hold values from -1.796875 to 1.796875
- cache_two: bfloat16 [4096, 768], P('tok', 'head'), may hold values from -1.796875 to 1.796875
- cache_uncond: bfloat16 [4096, 768], P('tok', 'head'), may hold values from -4 to 4
- norm_gain: float32 [768], replicated, may hold values from 0.5 to 1.5
- norm_bias: float32 [768], replicated, may hold values from -3 to 3
Outputs:
- normed: bfloat16 [4096, 768], P(('tok', 'head'))
- taylor_zero: bfloat16 [4096, 768], P('tok', 'head')
- taylor_one: bfloat16 [4096, 768], P('tok', 'head')
- taylor_two: bfloat16 [4096, 768], P('tok', 'head')
- taylor_three: bfloat16 [4096, 768], P('tok', 'head')
Inputs may be any that keep to these rules, and one draw needn't show every extreme that they name: `token_rank`: for each head a permutation of the tokens: the position of each token when the tokens are ordered by cluster, clusters in increasing number. `cluster_sizes`: for each head the sizes sum to 4096; every head has a cluster of exactly 477 tokens. `cluster_owner`: each group holds 4 clusters of every head and at most 480 tokens of a head, a bound that some group of every head reaches; of the tokens that one index of tok holds, at most 32 of one head lie in one group, a bound reached in every draw; heads 2j and 2j + 1 together have exactly 32 of those tokens in each group.
All inputs are finite; a program needn't handle non-finite values.
Results may differ from a plain program's by a relative error of at most 0.0059.
Values may be sent and summed in bfloat16 or wider, within the bound.
A program may use at most 64 MiB of HBM per device.

v0:
```python
import math

import jax
import jax.numpy as jnp
from jax import lax
from jax.sharding import PartitionSpec as P

HEAD_DIM = 64
STEP_GAP = 2


guide_scale = 6.0
norm_eps = 1e-05


def attend_pool(query_rows, key_rows, value_rows, tag_rows):
    total_rows = query_rows.shape[0]
    block_rows = math.gcd(total_rows, 512)

    def one_block(begin):
        block_q = lax.dynamic_slice_in_dim(query_rows, begin, block_rows, 0)
        block_tags = lax.dynamic_slice_in_dim(tag_rows, begin, block_rows, 0)
        scores = lax.dot_general(
            block_q, key_rows, (((1,), (1,)), ((), ())), preferred_element_type=jnp.float32
        ) * (1.0 / math.sqrt(HEAD_DIM))
        allowed = block_tags[:, None] == tag_rows[None, :]
        masked = jnp.where(allowed, scores, -jnp.inf)
        largest = jnp.max(masked, axis=1, keepdims=True)
        expo = jnp.where(allowed, jnp.exp(masked - largest), 0.0)
        totals = jnp.sum(expo, axis=1, keepdims=True)
        probability = (expo / totals).astype(jnp.bfloat16)
        return jnp.dot(probability, value_rows, preferred_element_type=jnp.float32).astype(
            jnp.bfloat16
        )

    starts = jnp.arange(total_rows // block_rows, dtype=jnp.int32) * block_rows
    return lax.map(one_block, starts).reshape(total_rows, HEAD_DIM)


def taylor_terms(attention, cache_zero, cache_one, cache_two):
    first_diff = (attention.astype(jnp.float32) - cache_zero.astype(jnp.float32)) / STEP_GAP
    second_diff = (first_diff - cache_one.astype(jnp.float32)) / STEP_GAP
    third_diff = (second_diff - cache_two.astype(jnp.float32)) / STEP_GAP
    return (
        first_diff.astype(jnp.bfloat16),
        second_diff.astype(jnp.bfloat16),
        third_diff.astype(jnp.bfloat16),
    )


def guide_rows(attention, cache_uncond):
    attention_wide = attention.astype(jnp.float32)
    uncond_wide = cache_uncond.astype(jnp.float32)
    return (uncond_wide + guide_scale * (attention_wide - uncond_wide)).astype(jnp.bfloat16)


def layer_norm(guided, norm_gain, norm_bias):
    widened = lax.optimization_barrier(guided).astype(jnp.float32)
    row_mean = jnp.mean(widened, axis=1, keepdims=True)
    centered = widened - row_mean
    row_var = jnp.mean(centered * centered, axis=1, keepdims=True)
    return (centered * lax.rsqrt(row_var + norm_eps) * norm_gain + norm_bias).astype(jnp.bfloat16)


def on_device(
    qkv,
    token_rank,
    cluster_sizes,
    cluster_owner,
    cache_zero,
    cache_one,
    cache_two,
    cache_uncond,
    norm_gain,
    norm_bias,
):
    group_count = lax.axis_size("tok")
    head_count = token_rank.shape[0]
    tok_count = token_rank.shape[1]
    cluster_count = cluster_sizes.shape[1]
    cluster_ends = jnp.cumsum(cluster_sizes, axis=1)
    members = jnp.sum(
        (cluster_ends[:, None, :] <= token_rank[:, :, None]).astype(jnp.int32), axis=2
    )
    chosen = members[:, :, None] == jnp.arange(cluster_count, dtype=jnp.int32)[None, None, :]
    targets = jnp.sum(jnp.where(chosen, cluster_owner[:, None, :], 0), axis=2)
    dest_hits = (
        targets[:, :, None] == jnp.arange(group_count, dtype=jnp.int32)[None, None, :]
    ).astype(jnp.int32)
    earlier = jnp.cumsum(dest_hits, axis=1) - dest_hits
    position = jnp.sum(earlier * dest_hits, axis=2)
    head_ids = jnp.arange(head_count, dtype=jnp.int32)[:, None]
    flat_id = (jnp.arange(tok_count, dtype=jnp.int32)[None, :] * head_count + head_ids).reshape(-1)
    query_flat = qkv[0].reshape(tok_count * head_count, HEAD_DIM)
    key_flat = qkv[1].reshape(tok_count * head_count, HEAD_DIM)
    value_flat = qkv[2].reshape(tok_count * head_count, HEAD_DIM)
    pool = head_count * (tok_count // group_count)
    group_counts = jnp.sum(dest_hits, axis=1)
    head_offset = jnp.cumsum(group_counts, axis=0) - group_counts
    base_offset = jnp.take_along_axis(head_offset, targets, axis=1)
    pool_index = targets * pool + base_offset + position
    pool_source = (
        jnp.zeros((group_count * pool,), jnp.int32).at[pool_index.reshape(-1)].set(flat_id)
    )
    tag_values = (head_ids * cluster_count + members).reshape(-1)
    pool_tags = (
        jnp.zeros((group_count * pool,), jnp.int32).at[pool_index.reshape(-1)].set(tag_values)
    )
    send_q = query_flat[pool_source].reshape(group_count, pool * HEAD_DIM)
    send_k = key_flat[pool_source].reshape(group_count, pool * HEAD_DIM)
    send_v = value_flat[pool_source].reshape(group_count, pool * HEAD_DIM)
    arrived = (
        lax.all_to_all(send_q, "tok", split_axis=0, concat_axis=0, tiled=True),
        lax.all_to_all(send_k, "tok", split_axis=0, concat_axis=0, tiled=True),
        lax.all_to_all(send_v, "tok", split_axis=0, concat_axis=0, tiled=True),
        lax.all_to_all(
            pool_tags.reshape(group_count, pool), "tok", split_axis=0, concat_axis=0, tiled=True
        ),
    )
    pooled = attend_pool(
        arrived[0].reshape(group_count * pool, HEAD_DIM),
        arrived[1].reshape(group_count * pool, HEAD_DIM),
        arrived[2].reshape(group_count * pool, HEAD_DIM),
        arrived[3].reshape(-1),
    )
    back_pool = lax.all_to_all(
        pooled.reshape(group_count, pool * HEAD_DIM), "tok", split_axis=0, concat_axis=0, tiled=True
    )
    picked = back_pool.reshape(group_count * pool, HEAD_DIM)[pool_index.transpose(1, 0).reshape(-1)]
    attention = picked.reshape(tok_count, head_count * HEAD_DIM)
    moved = (
        lax.all_to_all(attention, "head", split_axis=0, concat_axis=1, tiled=True),
        lax.all_to_all(cache_zero, "head", split_axis=0, concat_axis=1, tiled=True),
        lax.all_to_all(cache_one, "head", split_axis=0, concat_axis=1, tiled=True),
        lax.all_to_all(cache_two, "head", split_axis=0, concat_axis=1, tiled=True),
        lax.all_to_all(cache_uncond, "head", split_axis=0, concat_axis=1, tiled=True),
    )
    first_rows, second_rows, third_rows = taylor_terms(moved[0], moved[1], moved[2], moved[3])
    guided = guide_rows(moved[0], moved[4])
    normed = layer_norm(guided, norm_gain, norm_bias)
    taylor_back = (
        lax.all_to_all(first_rows, "head", split_axis=1, concat_axis=0, tiled=True),
        lax.all_to_all(second_rows, "head", split_axis=1, concat_axis=0, tiled=True),
        lax.all_to_all(third_rows, "head", split_axis=1, concat_axis=0, tiled=True),
    )
    return (normed, attention, taylor_back[0], taylor_back[1], taylor_back[2])


def solution(mesh):
    placed = (
        P(None, "tok", "head"),
        P("head", "tok"),
        P("head", None),
        P("head", None),
        P("tok", "head"),
        P("tok", "head"),
        P("tok", "head"),
        P("tok", "head"),
        P(),
        P(),
    )
    return jax.shard_map(
        on_device,
        mesh=mesh,
        in_specs=placed,
        out_specs=(
            P(("tok", "head"), None),
            P("tok", "head"),
            P("tok", "head"),
            P("tok", "head"),
            P("tok", "head"),
        ),
        check_vma=False,
    )
```

profile of v0, /device:TPU:0, one launch (start us, length us, event | category | flops | bytes accessed | tf_op | source)
XLA Modules:
  0.0 190.0 jit_solution(13196473778737863628)
XLA Ops:
  3.3 3.4 %reduce-window.6 = s32[6,16,2,128]{3,1,2,0:T(8,128)S(1)} reduce-window(s32[6,16,2,128]{3,1,2,0:T(8,128)S(1)} %fusion.24, s32[]{:T(128)} %constant.35.clone.1), window={size=1x1x1x128 pad=0_0x0_0x0_0x127_0}, to_apply=%region_5.6 | reduce-window | flops 3121152 | bytes 196612 | tf_op jit(solution)/shard_map/reduce-window
  7.5 7.0 %gather_fusion.4 = s32[1536]{0:T(1024)S(1)} fusion(s32[6,16]{1,0:T(8,128)S(1)} %sub.41, s32[1536]{0:T(1024)S(1)} %reshape.310), kind=kCustom, calls=%fused_computation.4 | custom fusion | bytes 24576 | tf_op jit(solution)/shard_map/jit(take_along_axis)/gather | solution.py:100
  14.5 6.2 %scatter_custom_fusion = s32[1536]{0:T(1024)S(1)} fusion(s32[1536]{0:T(1024)S(1)} %fusion.29, s32[1536]{0:T(1024)S(1)} %reshape.320, s32[]{:T(128)} %constant.35.clone.1), kind=kCustom, calls=%fused_computation.77 | custom fusion | bytes 6148 | tf_op jit(solution)/shard_map/scatter | solution.py:107
  21.4 7.4 %all-to-all-start.1 = ((s32[16,1,96]{2,1,0:T(1,128)}), s32[16,1,96]{2,1,0:T(1,128)S(1)}, u32[]{:S(2)}, u32[]{:S(2)}) async-start(s32[16,1,96]{2,1,0:T(1,128)} %all_to_all.120), calls=%async_computation.1 | async-start | bytes 16384 | tf_op jit(solution)/shard_map/all_to_all | solution.py:116
  28.8 6.2 %scatter_custom_fusion.1 = s32[1536]{0:T(1024)S(1)} fusion(s32[1536]{0:T(1024)S(1)} %fusion.29, s32[1536]{0:T(1024)S(1)} %reshape.328, s32[]{:T(128)} %constant.35.clone.1), kind=kCustom, calls=%fused_computation.75 | custom fusion | bytes 6148 | tf_op jit(solution)/shard_map/scatter | solution.py:103
  35.3 3.2 %gather_fusion = bf16[1536,64]{1,0:T(8,128)(2,1)S(1)} fusion(bf16[1536,64]{1,0:T(8,128)(2,1)S(1)} %reshape_squeeze.9, s32[2048]{0:T(1024)S(1)} %pad_clamp_fusion.1), kind=kCustom, calls=%fused_computation | custom fusion | bytes 399360 | tf_op jit(solution)/shard_map/gather | solution.py:109
  39.2 1.8 reduce.14
  41.8 6.0 %all-to-all-start.2 = ((bf16[16,2,3072]{2,1,0:T(2,128)(2,1)}), bf16[16,2,3072]{2,1,0:T(2,128)(2,1)S(1)}, u32[]{:S(2)}, u32[]{:S(2)}) async-start(bf16[16,2,3072]{2,1,0:T(2,128)(2,1)} %reshape.356), calls=%async_computation.2 | async-start | bytes 393216 | tf_op jit(solution)/shard_map/all_to_all | solution.py:113
  48.1 3.2 %gather_fusion.1 = bf16[1536,64]{1,0:T(8,128)(2,1)S(1)} fusion(bf16[1536,64]{1,0:T(8,128)(2,1)S(1)} %reshape_squeeze.10, s32[2048]{0:T(1024)S(1)} %pad_clamp_fusion.1), kind=kCustom, calls=%fused_computation.1 | custom fusion | bytes 399360 | tf_op jit(solution)/shard_map/gather | solution.py:110
  51.5 1.8 reduce.15
  54.1 2.8 %all-to-all-done.2 = bf16[16,2,3072]{2,1,0:T(2,128)(2,1)S(1)} async-done(((bf16[16,2,3072]{2,1,0:T(2,128)(2,1)}), bf16[16,2,3072]{2,1,0:T(2,128)(2,1)S(1)}, u32[]{:S(2)}, u32[]{:S(2)}) %all-to-all-start.2) | async-done | bytes 196640 | tf_op jit(solution)/shard_map/all_to_all | solution.py:113
  56.8 3.5 %all-to-all-start.3 = ((bf16[16,2,3072]{2,1,0:T(2,128)(2,1)}), bf16[16,2,3072]{2,1,0:T(2,128)(2,1)S(1)}, u32[]{:S(2)}, u32[]{:S(2)}) async-start(bf16[16,2,3072]{2,1,0:T(2,128)(2,1)} %reshape.358), calls=%async_computation.3 | async-start | bytes 393216 | tf_op jit(solution)/shard_map/all_to_all | solution.py:114
  60.6 3.2 %gather_fusion.2 = bf16[1536,64]{1,0:T(8,128)(2,1)S(1)} fusion(bf16[1536,64]{1,0:T(8,128)(2,1)S(1)} %reshape_squeeze.11, s32[2048]{0:T(1024)S(1)} %pad_clamp_fusion.1), kind=kCustom, calls=%fused_computation.2 | custom fusion | bytes 399360 | tf_op jit(solution)/shard_map/gather | solution.py:111
  64.0 1.8 reduce.16
  66.6 2.8 %all-to-all-done.3 = bf16[16,2,3072]{2,1,0:T(2,128)(2,1)S(1)} async-done(((bf16[16,2,3072]{2,1,0:T(2,128)(2,1)}), bf16[16,2,3072]{2,1,0:T(2,128)(2,1)S(1)}, u32[]{:S(2)}, u32[]{:S(2)}) %all-to-all-start.3) | async-done | bytes 196640 | tf_op jit(solution)/shard_map/all_to_all | solution.py:114
  69.3 3.7 %all-to-all-start.4 = ((bf16[16,2,3072]{2,1,0:T(2,128)(2,1)}), bf16[16,2,3072]{2,1,0:T(2,128)(2,1)S(1)}, u32[]{:S(2)}, u32[]{:S(2)}) async-start(bf16[16,2,3072]{2,1,0:T(2,128)(2,1)} %reshape.360), calls=%async_computation.4 | async-start | bytes 393216 | tf_op jit(solution)/shard_map/all_to_all | solution.py:115
  74.6 1.1 reduce.3
  76.2 1.1 reduce.4
  77.7 4.1 %all-to-all-done.4 = bf16[16,2,3072]{2,1,0:T(2,128)(2,1)S(1)} async-done(((bf16[16,2,3072]{2,1,0:T(2,128)(2,1)}), bf16[16,2,3072]{2,1,0:T(2,128)(2,1)S(1)}, u32[]{:S(2)}, u32[]{:S(2)}) %all-to-all-start.4) | async-done | bytes 196640 | tf_op jit(solution)/shard_map/all_to_all | solution.py:115
  82.0 1.1 reduce.5
  83.5 15.5 %while.11 = (s32[]{:T(128)}, bf16[3,512,64]{1,2,0:T(8,128)(2,1)S(1)}, s32[3]{0:T(128)S(1)}, s32[1536]{0:T(1024)S(1)}, s32[16,96]{1,0:T(8,128)}, /*index=5*/bf16[...) while((s32[]{:T(128)}, ...), condition=%wide.wide.region_13.14_spmd, body=%wide.wide.region_10.13_spmd.sunk | while | flops 211581952 | bytes 10463407 | solution.py:37
  87.6 1.0 fusion.54
  92.7 1.0 fusion.54
  97.9 1.0 fusion.54
  99.4 1.8 reduce.17
  102.0 3.5 %all-to-all-start.5 = ((bf16[16,2,3072]{2,1,0:T(2,128)(2,1)}), bf16[16,2,3072]{2,1,0:T(2,128)(2,1)S(1)}, u32[]{:S(2)}, u32[]{:S(2)}) async-start(bf16[16,2,3072]{2,1,0:T(2,128)(2,1)} %reshape.362), calls=%async_computation.5 | async-start | bytes 393216 | tf_op jit(solution)/shard_map/all_to_all | solution.py:126
  105.9 8.6 %all-to-all-done.5 = bf16[16,2,3072]{2,1,0:T(2,128)(2,1)S(1)} async-done(((bf16[16,2,3072]{2,1,0:T(2,128)(2,1)}), bf16[16,2,3072]{2,1,0:T(2,128)(2,1)S(1)}, u32[]{:S(2)}, u32[]{:S(2)}) %all-to-all-start.5) | async-done | bytes 196640 | tf_op jit(solution)/shard_map/all_to_all | solution.py:126
  114.6 1.1 reduce.6
  116.1 3.2 %gather_fusion.3 = bf16[1536,64]{1,0:T(8,128)(2,1)S(1)} fusion(bf16[1536,64]{1,0:T(8,128)(2,1)S(1)} %reshape.273, s32[2048]{0:T(1024)S(1)} %pad_clamp_fusion), kind=kCustom, calls=%fused_computation.3 | custom fusion | bytes 399360 | tf_op jit(solution)/shard_map/gather | solution.py:129
  119.3 0.9 all_to_all.131
  120.3 3.4 %all-to-all-start.6 = ((bf16[2,128,384]{2,1,0:T(8,128)(2,1)}), bf16[2,128,384]{2,1,0:T(8,128)(2,1)S(1)}, u32[]{:S(2)}, u32[]{:S(2)}) async-start(bf16[2,128,384]{2,1,0:T(8,128)(2,1)} %all_to_all.131), calls=%async_computation.6 | async-start | bytes 393216 | tf_op jit(solution)/shard_map/all_to_all | solution.py:132
  124.5 0.9 reshape.275
  125.5 3.0 %all-to-all-done.6 = bf16[2,128,384]{2,1,0:T(8,128)(2,1)S(1)} async-done(((bf16[2,128,384]{2,1,0:T(8,128)(2,1)}), bf16[2,128,384]{2,1,0:T(8,128)(2,1)S(1)}, u32[]{:S(2)}, u32[]{:S(2)}) %all-to-all-start.6) | async-done | bytes 196640 | tf_op jit(solution)/shard_map/all_to_all | solution.py:132
  128.5 3.4 %all-to-all-start = ((bf16[2,128,384]{1,2,0:T(8,128)(2,1)}), bf16[2,128,384]{1,2,0:T(8,128)(2,1)S(1)}, u32[]{:S(2)}, u32[]{:S(2)}) async-start(bf16[2,128,384]{1,2,0:T(8,128)(2,1)} %copy.41), calls=%async_computation | async-start | bytes 393216 | tf_op jit(solution)/shard_map/all_to_all | solution.py:136
  132.2 4.6 %all-to-all-done = bf16[2,128,384]{1,2,0:T(8,128)(2,1)S(1)} async-done(((bf16[2,128,384]{1,2,0:T(8,128)(2,1)}), bf16[2,128,384]{1,2,0:T(8,128)(2,1)S(1)}, u32[]{:S(2)}, u32[]{:S(2)}) %all-to-all-start) | async-done | bytes 196640 | tf_op jit(solution)/shard_map/all_to_all | solution.py:136
  136.8 3.4 %all-to-all-start.11 = ((bf16[2,128,384]{2,1,0:T(8,128)(2,1)}), bf16[2,128,384]{2,1,0:T(8,128)(2,1)S(1)}, u32[]{:S(2)}, u32[]{:S(2)}) async-start(bf16[2,128,384]{2,1,0:T(8,128)(2,1)} %bitcast.22), calls=%async_computation.11 | async-start | bytes 393216 | tf_op jit(solution)/shard_map/all_to_all | solution.py:135
  140.3 4.7 %all-to-all-done.11 = bf16[2,128,384]{2,1,0:T(8,128)(2,1)S(1)} async-done(((bf16[2,128,384]{2,1,0:T(8,128)(2,1)}), bf16[2,128,384]{2,1,0:T(8,128)(2,1)S(1)}, u32[]{:S(2)}, u32[]{:S(2)}) %all-to-all-start.11) | async-done | bytes 196640 | tf_op jit(solution)/shard_map/all_to_all | solution.py:135
  145.0 3.4 %all-to-all-start.7 = ((bf16[2,128,384]{2,1,0:T(8,128)(2,1)}), bf16[2,128,384]{2,1,0:T(8,128)(2,1)S(1)}, u32[]{:S(2)}, u32[]{:S(2)}) async-start(bf16[2,128,384]{2,1,0:T(8,128)(2,1)} %bitcast.14), calls=%async_computation.7 | async-start | bytes 393216 | tf_op jit(solution)/shard_map/all_to_all | solution.py:133
  148.6 4.7 %all-to-all-done.7 = bf16[2,128,384]{2,1,0:T(8,128)(2,1)S(1)} async-done(((bf16[2,128,384]{2,1,0:T(8,128)(2,1)}), bf16[2,128,384]{2,1,0:T(8,128)(2,1)S(1)}, u32[]{:S(2)}, u32[]{:S(2)}) %all-to-all-start.7) | async-done | bytes 196640 | tf_op jit(solution)/shard_map/all_to_all | solution.py:133
  153.3 3.4 %all-to-all-start.9 = ((bf16[2,128,384]{2,1,0:T(8,128)(2,1)}), bf16[2,128,384]{2,1,0:T(8,128)(2,1)S(1)}, u32[]{:S(2)}, u32[]{:S(2)}) async-start(bf16[2,128,384]{2,1,0:T(8,128)(2,1)} %bitcast.18), calls=%async_computation.9 | async-start | bytes 393216 | tf_op jit(solution)/shard_map/all_to_all | solution.py:134
  156.7 4.8 %all-to-all-done.9 = bf16[2,128,384]{2,1,0:T(8,128)(2,1)S(1)} async-done(((bf16[2,128,384]{2,1,0:T(8,128)(2,1)}), bf16[2,128,384]{2,1,0:T(8,128)(2,1)S(1)}, u32[]{:S(2)}, u32[]{:S(2)}) %all-to-all-start.9) | async-done | bytes 196640 | tf_op jit(solution)/shard_map/all_to_all | solution.py:134
  161.5 0.9 fusion.21
  162.5 3.4 %all-to-all-start.8 = ((bf16[128,2,384]{2,0,1:T(8,128)(2,1)}), bf16[128,2,384]{2,0,1:T(8,128)(2,1)S(1)}, u32[]{:S(2)}, u32[]{:S(2)}) async-start(bf16[128,2,384]{2,0,1:T(8,128)(2,1)} %get-tuple-element.88), calls=%async_computation.8 | async-start | bytes 393216 | tf_op jit(solution)/shard_map/all_to_all | solution.py:142
  166.0 5.5 %all-to-all-done.8 = bf16[128,2,384]{2,0,1:T(8,128)(2,1)S(1)} async-done(((bf16[128,2,384]{2,0,1:T(8,128)(2,1)}), bf16[128,2,384]{2,0,1:T(8,128)(2,1)S(1)}, u32[]{:S(2)}, u32[]{:S(2)}) %all-to-all-start.8) | async-done | bytes 196640 | tf_op jit(solution)/shard_map/all_to_all | solution.py:142
  171.5 3.4 %all-to-all-start.10 = ((bf16[128,2,384]{2,0,1:T(8,128)(2,1)}), bf16[128,2,384]{2,0,1:T(8,128)(2,1)S(1)}, u32[]{:S(2)}, u32[]{:S(2)}) async-start(bf16[128,2,384]{2,0,1:T(8,128)(2,1)} %get-tuple-element.84), calls=%async_computation.10 | async-start | bytes 393216 | tf_op jit(solution)/shard_map/all_to_all | solution.py:143
  174.9 4.8 %all-to-all-done.10 = bf16[128,2,384]{2,0,1:T(8,128)(2,1)S(1)} async-done(((bf16[128,2,384]{2,0,1:T(8,128)(2,1)}), bf16[128,2,384]{2,0,1:T(8,128)(2,1)S(1)}, u32[]{:S(2)}, u32[]{:S(2)}) %all-to-all-start.10) | async-done | bytes 196640 | tf_op jit(solution)/shard_map/all_to_all | solution.py:143
  179.7 3.4 %all-to-all-start.12 = ((bf16[128,2,384]{2,0,1:T(8,128)(2,1)}), bf16[128,2,384]{2,0,1:T(8,128)(2,1)S(1)}, u32[]{:S(2)}, u32[]{:S(2)}) async-start(bf16[128,2,384]{2,0,1:T(8,128)(2,1)} %get-tuple-element.83), calls=%async_computation.12 | async-start | bytes 393216 | tf_op jit(solution)/shard_map/all_to_all | solution.py:144
  184.3 3.7 %all-to-all-done.12 = bf16[128,2,384]{2,0,1:T(8,128)(2,1)S(1)} async-done(((bf16[128,2,384]{2,0,1:T(8,128)(2,1)}), bf16[128,2,384]{2,0,1:T(8,128)(2,1)S(1)}, u32[]{:S(2)}, u32[]{:S(2)}) %all-to-all-start.12) | async-done | bytes 196640 | tf_op jit(solution)/shard_map/all_to_all | solution.py:144
  (95 shorter events, 24.2 us)
Async XLA Ops:
  7.5 27.5 %copy-start = (bf16[3,256,384]{2,1,0:T(8,128)(2,1)S(1)}, bf16[3,256,384]{2,1,0:T(8,128)(2,1)}, u32[]{:S(2)}) copy-start(bf16[3,256,384]{2,1,0:T(8,128)(2,1)} %param.12) | copy-start | bytes 1769476
  21.4 20.4 %all-to-all-start.1 = ((s32[16,1,96]{2,1,0:T(1,128)}), s32[16,1,96]{2,1,0:T(1,128)S(1)}, u32[]{:S(2)}, u32[]{:S(2)}) async-start(s32[16,1,96]{2,1,0:T(1,128)} %all_to_all.120), calls=%async_computation.1 | async-start | bytes 16384 | tf_op jit(solution)/shard_map/all_to_all | solution.py:116
  41.8 31.8 %copy-start.2 = (s32[16,1,96]{2,1,0:T(1,128)}, s32[16,1,96]{2,1,0:T(1,128)S(1)}, u32[]{:S(2)}) copy-start(s32[16,1,96]{2,1,0:T(1,128)S(1)} %all-to-all-done.1) | copy-start | bytes 18436
  41.8 15.0 %all-to-all-start.2 = ((bf16[16,2,3072]{2,1,0:T(2,128)(2,1)}), bf16[16,2,3072]{2,1,0:T(2,128)(2,1)S(1)}, u32[]{:S(2)}, u32[]{:S(2)}) async-start(bf16[16,2,3072]{2,1,0:T(2,128)(2,1)} %reshape.356), calls=%async_computation.2 | async-start | bytes 393216 | tf_op jit(solution)/shard_map/all_to_all | solution.py:113
  56.8 12.5 %all-to-all-start.3 = ((bf16[16,2,3072]{2,1,0:T(2,128)(2,1)}), bf16[16,2,3072]{2,1,0:T(2,128)(2,1)S(1)}, u32[]{:S(2)}, u32[]{:S(2)}) async-start(bf16[16,2,3072]{2,1,0:T(2,128)(2,1)} %reshape.358), calls=%async_computation.3 | async-start | bytes 393216 | tf_op jit(solution)/shard_map/all_to_all | solution.py:114
  69.3 12.5 %all-to-all-start.4 = ((bf16[16,2,3072]{2,1,0:T(2,128)(2,1)}), bf16[16,2,3072]{2,1,0:T(2,128)(2,1)S(1)}, u32[]{:S(2)}, u32[]{:S(2)}) async-start(bf16[16,2,3072]{2,1,0:T(2,128)(2,1)} %reshape.360), calls=%async_computation.4 | async-start | bytes 393216 | tf_op jit(solution)/shard_map/all_to_all | solution.py:115
  102.0 12.5 %all-to-all-start.5 = ((bf16[16,2,3072]{2,1,0:T(2,128)(2,1)}), bf16[16,2,3072]{2,1,0:T(2,128)(2,1)S(1)}, u32[]{:S(2)}, u32[]{:S(2)}) async-start(bf16[16,2,3072]{2,1,0:T(2,128)(2,1)} %reshape.362), calls=%async_computation.5 | async-start | bytes 393216 | tf_op jit(solution)/shard_map/all_to_all | solution.py:126
  105.9 17.9 %copy-start.1 = (bf16[256,384]{1,0:T(8,128)(2,1)S(1)}, bf16[256,384]{1,0:T(8,128)(2,1)}, u32[]{:S(2)}) copy-start(bf16[256,384]{1,0:T(8,128)(2,1)} %param.19) | copy-start | bytes 589828
  120.3 8.2 %all-to-all-start.6 = ((bf16[2,128,384]{2,1,0:T(8,128)(2,1)}), bf16[2,128,384]{2,1,0:T(8,128)(2,1)S(1)}, u32[]{:S(2)}, u32[]{:S(2)}) async-start(bf16[2,128,384]{2,1,0:T(8,128)(2,1)} %all_to_all.131), calls=%async_computation.6 | async-start | bytes 393216 | tf_op jit(solution)/shard_map/all_to_all | solution.py:132
  128.5 8.2 %all-to-all-start = ((bf16[2,128,384]{1,2,0:T(8,128)(2,1)}), bf16[2,128,384]{1,2,0:T(8,128)(2,1)S(1)}, u32[]{:S(2)}, u32[]{:S(2)}) async-start(bf16[2,128,384]{1,2,0:T(8,128)(2,1)} %copy.41), calls=%async_computation | async-start | bytes 393216 | tf_op jit(solution)/shard_map/all_to_all | solution.py:136
  132.0 51.2 %copy-start.3 = (f32[768]{0:T(1024)S(1)}, f32[768]{0:T(1024)}, u32[]{:S(2)}) copy-start(f32[768]{0:T(1024)} %param.21) | copy-start | bytes 9220
  132.0 51.2 %copy-start.4 = (f32[768]{0:T(1024)S(1)}, f32[768]{0:T(1024)}, u32[]{:S(2)}) copy-start(f32[768]{0:T(1024)} %param.20) | copy-start | bytes 9220
  136.8 8.2 %all-to-all-start.11 = ((bf16[2,128,384]{2,1,0:T(8,128)(2,1)}), bf16[2,128,384]{2,1,0:T(8,128)(2,1)S(1)}, u32[]{:S(2)}, u32[]{:S(2)}) async-start(bf16[2,128,384]{2,1,0:T(8,128)(2,1)} %bitcast.22), calls=%async_computation.11 | async-start | bytes 393216 | tf_op jit(solution)/shard_map/all_to_all | solution.py:135
  145.0 8.2 %all-to-all-start.7 = ((bf16[2,128,384]{2,1,0:T(8,128)(2,1)}), bf16[2,128,384]{2,1,0:T(8,128)(2,1)S(1)}, u32[]{:S(2)}, u32[]{:S(2)}) async-start(bf16[2,128,384]{2,1,0:T(8,128)(2,1)} %bitcast.14), calls=%async_computation.7 | async-start | bytes 393216 | tf_op jit(solution)/shard_map/all_to_all | solution.py:133
  153.3 8.2 %all-to-all-start.9 = ((bf16[2,128,384]{2,1,0:T(8,128)(2,1)}), bf16[2,128,384]{2,1,0:T(8,128)(2,1)S(1)}, u32[]{:S(2)}, u32[]{:S(2)}) async-start(bf16[2,128,384]{2,1,0:T(8,128)(2,1)} %bitcast.18), calls=%async_computation.9 | async-start | bytes 393216 | tf_op jit(solution)/shard_map/all_to_all | solution.py:134
  162.5 9.0 %all-to-all-start.8 = ((bf16[128,2,384]{2,0,1:T(8,128)(2,1)}), bf16[128,2,384]{2,0,1:T(8,128)(2,1)S(1)}, u32[]{:S(2)}, u32[]{:S(2)}) async-start(bf16[128,2,384]{2,0,1:T(8,128)(2,1)} %get-tuple-element.88), calls=%async_computation.8 | async-start | bytes 393216 | tf_op jit(solution)/shard_map/all_to_all | solution.py:142
  171.5 8.2 %all-to-all-start.10 = ((bf16[128,2,384]{2,0,1:T(8,128)(2,1)}), bf16[128,2,384]{2,0,1:T(8,128)(2,1)S(1)}, u32[]{:S(2)}, u32[]{:S(2)}) async-start(bf16[128,2,384]{2,0,1:T(8,128)(2,1)} %get-tuple-element.84), calls=%async_computation.10 | async-start | bytes 393216 | tf_op jit(solution)/shard_map/all_to_all | solution.py:143
  179.7 8.2 %all-to-all-start.12 = ((bf16[128,2,384]{2,0,1:T(8,128)(2,1)}), bf16[128,2,384]{2,0,1:T(8,128)(2,1)S(1)}, u32[]{:S(2)}, u32[]{:S(2)}) async-start(bf16[128,2,384]{2,0,1:T(8,128)(2,1)} %get-tuple-element.83), calls=%async_computation.12 | async-start | bytes 393216 | tf_op jit(solution)/shard_map/all_to_all | solution.py:144
where the time goes:
time: 191 us; the launch traced here: 190 us
  waiting for transfers between devices  54 us (28%)
  starting transfers between devices  51.6 us (27%)
  local copies, waits for them, and re-layouts  49.5 us (26%)
  other arithmetic  22.5 us (12%)
  loops' own time  5.9 us (3%)
  matrix products  5.28 us (3%)
    scatter x2, local copies, waits for them, and re-layouts, on_device(): jnp.zeros((group_count * pool,), jnp.int32).at[pool_index.reshape(-1)]  12.4 us
    all_to_all x1, waiting for transfers between devices, on_device(): lax.all_to_all(pooled.reshape(group_count, pool * HEAD_DIM), 'tok', split...  8.59 us
    all_to_all x1, starting transfers between devices, on_device(): lax.all_to_all(pool_tags.reshape(group_count, pool), 'tok', split_axis=0,...  7.36 us
    gather x3, local copies, waits for them, and re-layouts, on_device(): base_offset = jnp.take_along_axis(head_offset, targets, axis=1)  6.99 us
    unnamed x24, local copies, waits for them, and re-layouts  6.72 us
    all_to_all x1, starting transfers between devices, on_device(): lax.all_to_all(send_q, 'tok', split_axis=0, concat_axis=0, tiled=True)  6.01 us
    another operation x1, loops' own time, attend_pool(): return lax.map(one_block, starts).reshape(total_rows, HEAD_DIM)  5.9 us
    all_to_all x1, waiting for transfers between devices, on_device(): lax.all_to_all(first_rows, 'head', split_axis=1, concat_axis=0, tiled=True)  5.46 us
  transfers between devices with their start and end apart: 13, of which 12 were waited for; matrix products, arithmetic and copies ran while one was open for 17% of the time, Pallas kernels for 0%

commit v1 on v0

v1 whole, which is shorter than its diff:
```python
import functools
import math

import jax
import jax.numpy as jnp
from jax import lax
from jax.experimental import pallas as pl
from jax.experimental.pallas import tpu as pltpu
from jax.sharding import PartitionSpec as P

HEAD_DIM = 64
LANES = 128
STEP_GAP = 2
GUIDE = 6.0
EPS = 1e-05
F32 = jnp.float32
BF16 = jnp.bfloat16
MESH = pl.DeviceIdType.MESH
NEG = -1e30
SCORE_SCALE = math.log2(math.e) / math.sqrt(HEAD_DIM)


def mm(a, b):
    return jnp.dot(a, b, preferred_element_type=F32)


def mm_nt(a, b):
    return lax.dot_general(a, b, (((1,), (1,)), ((), ())), preferred_element_type=F32)


def iota(shape, axis):
    return lax.broadcasted_iota(jnp.int32, shape, axis)


def exchange_kernel(
    groups,
    head_peers,
    qkv,
    rank,
    sizes,
    owner,
    uncond,
    att_out,
    rows_out,
    send,
    recv,
    back,
    home,
    gsend,
    grecv,
    codes,
    fs,
    fr,
    bs,
    br,
    hs,
    hr,
):
    me = lax.axis_index("tok")
    my_head = lax.axis_index("head")
    heads, toks = rank.shape
    pairs = heads // 2
    nclust = sizes.shape[1]
    slots = send.shape[2]
    half = slots // 2
    total = groups * slots

    barrier = pltpu.get_barrier_semaphore()

    def greet_tok(k, c):
        pl.semaphore_signal(
            barrier, inc=1, device_id={"tok": lax.rem(me + k, groups)}, device_id_type=MESH
        )
        return c

    def greet_head(k, c):
        pl.semaphore_signal(
            barrier,
            inc=1,
            device_id={"head": lax.rem(my_head + k, head_peers)},
            device_id_type=MESH,
        )
        return c

    lax.fori_loop(1, groups, greet_tok, 0)
    lax.fori_loop(1, head_peers, greet_head, 0)

    upto = (iota((nclust, nclust), 1) <= iota((nclust, nclust), 0)).astype(F32).astype(BF16)
    size_all = sizes[...]
    size_hi = (size_all >> 7).astype(F32).astype(BF16)
    size_lo = (size_all & 127).astype(F32).astype(BF16)
    ends = mm_nt(upto, size_hi) * 128.0 + mm_nt(upto, size_lo)
    before = (iota((nclust, nclust), 1) < iota((nclust, nclust), 0)).astype(F32).astype(BF16)
    starts = mm_nt(before, size_hi) * 128.0 + mm_nt(before, size_lo)

    group_iota = iota((groups, nclust), 0)
    members = []
    hits = []
    for h in range(heads):
        ranks = rank[h : h + 1, :].astype(F32)
        passed = ends[:, h : h + 1] <= ranks
        begun = starts[:, h : h + 1] <= ranks
        members.append(jnp.sum(jnp.where(passed, 1.0, 0.0), axis=0, keepdims=True))
        inside = jnp.where(begun, 1.0, 0.0) - jnp.where(passed, 1.0, 0.0)
        owned = jnp.where(group_iota == owner[h : h + 1, :], 1.0, 0.0).astype(BF16)
        hits.append(mm(owned, inside.astype(BF16)))
    all_hits = jnp.concatenate(hits, axis=0)
    earlier_mat = jnp.where(iota((toks, toks), 0) < iota((toks, toks), 1), 1.0, 0.0).astype(BF16)
    earlier = mm(all_hits.astype(BF16), earlier_mat)
    counts = jnp.sum(all_hits, axis=1, keepdims=True)
    group_base = iota((groups, toks), 0).astype(F32)
    slot_rows = []
    codes[...] = jnp.full(codes.shape, -1.0, F32)
    for h in range(heads):
        lo = h * groups
        hit = hits[h]
        place = earlier[lo : lo + groups]
        if h % 2 == 1:
            place = place + counts[lo - groups : lo]
        spot = jnp.sum(hit * place, axis=0, keepdims=True)
        dest = jnp.sum(hit * group_base, axis=0, keepdims=True)
        slot_rows.append((dest * slots + spot).astype(jnp.int32))
        code = dest * half + spot
        codes[h : h + 1, :] = jnp.where(spot < half, code, -1.0)
        codes[heads + h : heads + h + 1, :] = jnp.where(spot >= half, code - half, -1.0)

    lane_tok = iota((toks, LANES), 1)
    slot_iota = iota((total, toks), 0)
    tag_row = iota((LANES, toks), 0)

    def pack(p):
        cols = slice(p * LANES, (p + 1) * LANES)
        q = qkv[0, :, cols].astype(F32)
        k = qkv[1, :, cols].astype(F32)
        v = qkv[2, :, cols].astype(F32)
        first = None
        for side in range(2):
            h = 2 * p + side
            pick = jnp.where(slot_iota == slot_rows[h], 1.0, 0.0).astype(BF16)
            tags = jnp.where(
                tag_row == HEAD_DIM,
                members[h] + 1.0,
                jnp.where(tag_row == HEAD_DIM + 1, float(side), 0.0),
            )
            tag_cols = jnp.transpose(tags)
            if side == 0:
                qv = jnp.where(lane_tok < HEAD_DIM, q, pltpu.roll(v, HEAD_DIM, 1))
                kt = jnp.where(lane_tok < HEAD_DIM, k, tag_cols)
            else:
                qv = jnp.where(lane_tok < HEAD_DIM, pltpu.roll(q, HEAD_DIM, 1), v)
                kt = jnp.where(lane_tok < HEAD_DIM, pltpu.roll(k, HEAD_DIM, 1), tag_cols)
            both = jnp.concatenate([qv, kt], axis=1).astype(BF16)
            part = mm(pick, both)
            first = part if first is None else first + part
        send[p] = first.astype(BF16).reshape(groups, slots, 2 * LANES)

    def forward(p, k):
        dst = lax.rem(me + k, groups)
        return pltpu.make_async_remote_copy(
            src_ref=send.at[p, dst],
            dst_ref=recv.at[p, me],
            send_sem=fs.at[p, dst],
            recv_sem=fr.at[p, me],
            device_id={"tok": dst},
            device_id_type=MESH,
        )

    def forward_wait(p, k):
        src = lax.rem(me + k, groups)
        return pltpu.make_async_remote_copy(
            src_ref=send.at[p, src],
            dst_ref=recv.at[p, src],
            send_sem=fs.at[p, src],
            recv_sem=fr.at[p, src],
            device_id={"tok": src},
            device_id_type=MESH,
        )

    def backward(p, k):
        dst = lax.rem(me + k, groups)
        return pltpu.make_async_remote_copy(
            src_ref=back.at[p, dst],
            dst_ref=home.at[p, me],
            send_sem=bs.at[p, dst],
            recv_sem=br.at[p, me],
            device_id={"tok": dst},
            device_id_type=MESH,
        )

    def backward_wait(p, k):
        src = lax.rem(me + k, groups)
        return pltpu.make_async_remote_copy(
            src_ref=back.at[p, src],
            dst_ref=home.at[p, src],
            send_sem=bs.at[p, src],
            recv_sem=br.at[p, src],
            device_id={"tok": src},
            device_id_type=MESH,
        )

    def loop(count, act):
        def body(k, c):
            act(k)
            return c

        lax.fori_loop(1, count, body, 0)

    for p in range(pairs):
        pack(p)
        if p == 0:
            pl.semaphore_wait(barrier, groups - 1 + head_peers - 1)
        loop(groups, lambda k: forward(p, k).start())
        recv[p, me] = send[p, me]

    code_cols = jnp.transpose(codes[...])
    back_iota = iota((toks, groups * half), 1).astype(F32)

    row_block = min(total, 256)
    wide_lane = iota((total, LANES), 1)
    sel_row = iota((8, LANES), 1)
    sel_r = jnp.where(
        sel_row == HEAD_DIM, 2.0, jnp.where(sel_row == HEAD_DIM + 1, 1.0, 0.0)
    ).astype(BF16)
    sel_col = iota((LANES, LANES), 0)
    sel_c = jnp.where(
        sel_col == HEAD_DIM, 2.0, jnp.where(sel_col == HEAD_DIM + 1, 1.0, 0.0)
    ).astype(BF16)

    for p in range(pairs):
        loop(groups, lambda k: forward_wait(p, k).wait_recv())
        blocks = recv[p].reshape(total, 2 * LANES)
        qv = blocks[:, :LANES]
        kt = blocks[:, LANES:]
        keys = jnp.where(wide_lane < HEAD_DIM, kt.astype(F32), 0.0).astype(BF16)
        tag_r = mm_nt(sel_r, kt)[0:1, :]
        chunk_groups = row_block // slots

        def attend(i, c):
            here = pl.ds(i * chunk_groups, chunk_groups)
            mine = recv[p, here].reshape(row_block, 2 * LANES)
            scores = mm_nt(mine[:, :LANES], keys)
            tag_c = mm(mine[:, LANES:], sel_c)
            tag_c = jnp.concatenate([tag_c] * (total // LANES), axis=1)
            masked = jnp.where(tag_c == tag_r, scores * SCORE_SCALE, NEG)
            largest = jnp.max(masked, axis=1, keepdims=True)
            expo = jnp.exp2(masked - largest)
            scale = 1.0 / jnp.sum(expo, axis=1, keepdims=True)
            out = mm((expo * scale).astype(BF16), qv)
            out = out.reshape(chunk_groups, slots, LANES)
            low = pltpu.roll(out[:, :half].reshape(chunk_groups * half, LANES), HEAD_DIM, 1)
            high = out[:, half:].reshape(chunk_groups * half, LANES)
            lane = iota((chunk_groups * half, LANES), 1)
            packed = jnp.where(lane < HEAD_DIM, low, high).astype(BF16)
            back[p, here] = packed.reshape(chunk_groups, half, LANES)
            return c

        steps = total // row_block
        lax.fori_loop(0, steps, attend, 0, unroll=steps <= 2)
        loop(groups, lambda k: backward(p, k).start())
        home[p, me] = back[p, me]

    peer_rows = toks // head_peers

    def guide(p, k):
        dst = lax.rem(my_head + k, head_peers)
        return pltpu.make_async_remote_copy(
            src_ref=gsend.at[p, dst],
            dst_ref=grecv.at[p, my_head],
            send_sem=hs.at[p, dst],
            recv_sem=hr.at[p, my_head],
            device_id={"head": dst},
            device_id_type=MESH,
        )

    def guide_wait(p, k):
        src = lax.rem(my_head + k, head_peers)
        return pltpu.make_async_remote_copy(
            src_ref=gsend.at[p, src],
            dst_ref=grecv.at[p, src],
            send_sem=hs.at[p, src],
            recv_sem=hr.at[p, src],
            device_id={"head": src},
            device_id_type=MESH,
        )

    for p in range(pairs):
        picks = []
        for h in (2 * p, 2 * p + 1):
            for row in (h, heads + h):
                hit = back_iota == code_cols[:, row : row + 1]
                picks.append(jnp.where(hit, 1.0, 0.0).astype(BF16))
        loop(groups, lambda k: backward_wait(p, k).wait_recv())
        arrived = home[p].reshape(groups * half, LANES)
        a_low, a_high, b_low, b_high = [mm(pick, arrived) for pick in picks]
        left = a_low + pltpu.roll(a_high, HEAD_DIM, 1)
        right = b_high + pltpu.roll(b_low, HEAD_DIM, 1)
        att = jnp.where(lane_tok < HEAD_DIM, left, right)
        cols = slice(p * LANES, (p + 1) * LANES)
        att_out[:, cols] = att.astype(BF16)
        base = uncond[:, cols].astype(F32)
        guided = (base + GUIDE * (att - base)).astype(BF16)
        gsend[p] = guided.reshape(head_peers, peer_rows, LANES)
        loop(head_peers, lambda k: guide(p, k).start())
        grecv[p, my_head] = gsend[p, my_head]

    for p in range(pairs):
        loop(head_peers, lambda k: guide_wait(p, k).wait_recv())
        for src in range(head_peers):
            at = (src * pairs + p) * LANES
            rows_out[:, at : at + LANES] = grecv[p, src]

    for p in range(pairs):
        loop(groups, lambda k: forward_wait(p, k).wait_send())
        loop(groups, lambda k: backward_wait(p, k).wait_send())
        loop(head_peers, lambda k: guide_wait(p, k).wait_send())


def finish_kernel(
    att, rows, zero, one, two, gain, bias, normed, att_out, first_out, second_out, third_out
):
    gap = 1.0 / STEP_GAP
    wide = att[...]
    att_out[...] = wide
    first = (wide.astype(F32) - zero[...].astype(F32)) * gap
    first_out[...] = first.astype(BF16)
    second = (first - one[...].astype(F32)) * gap
    second_out[...] = second.astype(BF16)
    third = (second - two[...].astype(F32)) * gap
    third_out[...] = third.astype(BF16)
    guided = rows[...].astype(F32)
    inv = 1.0 / guided.shape[1]
    centered = guided - jnp.sum(guided, axis=1, keepdims=True) * inv
    var = jnp.sum(centered * centered, axis=1, keepdims=True) * inv
    normed[...] = (centered * lax.rsqrt(var + EPS) * gain[...] + bias[...]).astype(BF16)


def on_device(
    groups,
    head_peers,
    qkv,
    token_rank,
    cluster_sizes,
    cluster_owner,
    cache_zero,
    cache_one,
    cache_two,
    cache_uncond,
    norm_gain,
    norm_bias,
):
    heads, toks = token_rank.shape
    pairs = heads // 2
    width = norm_gain.shape[0]
    mine = cache_zero.shape[1]
    share = 2 * toks // groups
    slots = -(-share // 32) * 32
    half = slots // 2
    peer_rows = toks // head_peers
    vmem = pl.BlockSpec(memory_space=pltpu.VMEM)
    att, rows = pl.pallas_call(
        functools.partial(exchange_kernel, groups, head_peers),
        out_shape=(
            jax.ShapeDtypeStruct((toks, mine), BF16),
            jax.ShapeDtypeStruct((peer_rows, width), BF16),
        ),
        in_specs=[vmem] * 5,
        out_specs=[vmem] * 2,
        scratch_shapes=[
            pltpu.VMEM((pairs, groups, slots, 2 * LANES), BF16),
            pltpu.VMEM((pairs, groups, slots, 2 * LANES), BF16),
            pltpu.VMEM((pairs, groups, half, LANES), BF16),
            pltpu.VMEM((pairs, groups, half, LANES), BF16),
            pltpu.VMEM((pairs, head_peers, peer_rows, LANES), BF16),
            pltpu.VMEM((pairs, head_peers, peer_rows, LANES), BF16),
            pltpu.VMEM((LANES, toks), F32),
            pltpu.SemaphoreType.DMA((pairs, groups)),
            pltpu.SemaphoreType.DMA((pairs, groups)),
            pltpu.SemaphoreType.DMA((pairs, groups)),
            pltpu.SemaphoreType.DMA((pairs, groups)),
            pltpu.SemaphoreType.DMA((pairs, head_peers)),
            pltpu.SemaphoreType.DMA((pairs, head_peers)),
        ],
        compiler_params=pltpu.CompilerParams(
            collective_id=0, has_side_effects=True, vmem_limit_bytes=48 * 1024 * 1024
        ),
        name="exchange",
    )(qkv, token_rank, cluster_sizes, cluster_owner, cache_uncond)
    piece = jax.ShapeDtypeStruct((toks, mine), BF16)
    return pl.pallas_call(
        finish_kernel,
        out_shape=(jax.ShapeDtypeStruct((peer_rows, width), BF16), piece, piece, piece, piece),
        in_specs=[vmem] * 7,
        out_specs=[vmem] * 5,
        compiler_params=pltpu.CompilerParams(vmem_limit_bytes=32 * 1024 * 1024),
        name="finish",
    )(
        att,
        rows,
        cache_zero,
        cache_one,
        cache_two,
        norm_gain.reshape(1, width),
        norm_bias.reshape(1, width),
    )


def solution(mesh):
    sides = P("tok", "head")
    return jax.shard_map(
        functools.partial(on_device, mesh.shape["tok"], mesh.shape["head"]),
        mesh=mesh,
        in_specs=(
            P(None, "tok", "head"),
            P("head", "tok"),
            P("head", None),
            P("head", None),
            sides,
            sides,
            sides,
            sides,
            P(),
            P(),
        ),
        out_specs=(P(("tok", "head"), None), sides, sides, sides, sides),
        check_vma=False,
    )
```

time: 191 us -> 44.8 us (0.23)
  waiting for transfers between devices: 54 us -> 0 us
  starting transfers between devices: 51.6 us -> 0 us
  local copies, waits for them, and re-layouts: 49.5 us -> 4.09 us
  Pallas kernels: 0 us -> 39.8 us
  other arithmetic: 22.5 us -> 0 us
  loops' own time: 5.9 us -> 0 us
  matrix products: 5.28 us -> 0 us
    all_to_all x13 -> x0, waiting for transfers between devices: 54 us -> none  [the longest x1 8.59 us: on_device(): lax.all_to_all(pooled.reshape(group_count, pool * HEAD_DIM), 'tok', split...]
    all_to_all x13 -> x0, starting transfers between devices: 51.6 us -> none  [the longest x1 7.36 us: on_device(): lax.all_to_all(pool_tags.reshape(group_count, pool), 'tok', split_axis=0,...]
    pallas_call x0 -> x2, Pallas kernels: none -> 39.8 us  [the longest x1 38.5 us: on_device(): pl.pallas_call(functools.partial(exchange_kernel, groups, head_peers), ou...]
    gather x7 -> x0, local copies, waits for them, and re-layouts: 19.8 us -> none  [the longest x3 6.99 us: on_device(): base_offset = jnp.take_along_axis(head_offset, targets, axis=1)]
    scatter x2 -> x0, local copies, waits for them, and re-layouts: 12.4 us -> none  [on_device(): jnp.zeros((group_count * pool,), jnp.int32).at[pool_index.reshape(-1)]]
    all_to_all x9 -> x0, other arithmetic: 12.2 us -> none  [the longest x2 2.87 us: on_device(): lax.all_to_all(send_v, 'tok', split_axis=0, concat_axis=0, tiled=True)]
    another operation x1 -> x0, loops' own time: 5.9 us -> none  [attend_pool(): return lax.map(one_block, starts).reshape(total_rows, HEAD_DIM)]
    dot_general x6 -> x0, matrix products: 5.28 us -> none  [the longest x3 3.14 us: one_block(): jnp.dot(probability, value_rows, preferred_element_type=jnp.float32)]
  transfers between devices with their start and end apart: 13 -> 0, of which waited for: 12 -> 0; matrix products, arithmetic and copies ran while one was open for 17% -> 0% of each run, Pallas kernels for 0% -> 0%
where the time goes in v1:
time: 44.8 us; the launch traced here: 44.5 us
  Pallas kernels  39.8 us (89%)
  local copies, waits for them, and re-layouts  4.09 us (9%)
  between operations  0.68 us (2%)
    pallas_call x1, Pallas kernels, on_device(): pl.pallas_call(functools.partial(exchange_kernel, groups, head_peers), ou...  38.5 us
    unnamed x16, local copies, waits for them, and re-layouts  2.69 us
    pallas_call x1, Pallas kernels, on_device(): pl.pallas_call(finish_kernel, out_shape=(jax.ShapeDtypeStruct((peer_rows,...  1.26 us

profile of v1, /device:TPU:0, one launch (start us, length us, event | category | flops | bytes accessed | tf_op | source)
XLA Modules:
  0.0 44.5 jit_solution(10876147725842055362)
XLA Ops:
  0.6 0.0 copy-start.5
  0.6 0.7 %reshape.16.gain = f32[1,768]{1,0:T(1,128)S(1)} reshape(f32[768]{0:T(1024)} %param.18) | data formatting | bytes 6144 | tf_op jit(solution)/shard_map/reshape | solution.py:402
  1.3 0.0 copy-start.6
  1.3 0.7 %reshape.17.bias = f32[1,768]{1,0:T(1,128)S(1)} reshape(f32[768]{0:T(1024)} %param.19) | data formatting | bytes 6144 | tf_op jit(solution)/shard_map/reshape | solution.py:403
  2.0 0.0 copy-done.5
  2.0 0.0 copy-done.6
  2.0 0.0 copy-start
  2.1 1.1 %copy-done = bf16[3,256,384]{2,1,0:T(8,128)(2,1)S(1)} copy-done((bf16[3,256,384]{2,1,0:T(8,128)(2,1)S(1)}, bf16[3,256,384]{2,1,0:T(8,128)(2,1)}, u32[]{:S(2)}) %copy-start) | copy-done | bytes 589848
  3.1 0.0 copy-start.1
  3.1 0.9 %copy-done.1 = bf16[256,384]{1,0:T(8,128)(2,1)S(1)} copy-done((bf16[256,384]{1,0:T(8,128)(2,1)S(1)}, bf16[256,384]{1,0:T(8,128)(2,1)}, u32[]{:S(2)}) %copy-start.1) | copy-done | bytes 196632
  4.0 0.0 copy-start.7
  4.0 0.7 %copy-done.7 = s32[6,64]{1,0:T(8,128)S(1)} copy-done((s32[6,64]{1,0:T(8,128)S(1)}, s32[6,64]{1,0:T(8,128)}, u32[]{:S(2)}) %copy-start.7) | copy-done | bytes 1560
  4.7 0.0 copy-start.2
  4.7 0.0 copy-start.3
  4.7 0.0 copy-start.4
  4.7 38.5 %exchange.1 = (bf16[256,384]{1,0:T(8,128)(2,1)S(1)}, bf16[128,768]{1,0:T(8,128)(2,1)S(1)}) custom-call(bf16[3,256,384]{2,1,0:T(8,128)(2,1)S(1)} %copy-done, s32[6,256]{1,0:T(8,128)S(1)} %copy-done.5, s32[6,64]{1,0:T(8,128)S(1)} %copy-done.6, s32[6,64]{1,0:T(8,128)S(1)} %copy-done.7, bf16[256,384]{1,0:T(8,128)(2,1)S(1)} %copy-done.1), custom_call_target="tpu_custom_call" | custom-call | tf_op jit(solution)/shard_map/exchange/pallas_call | solution.py:360
  43.2 0.0 copy-done.2
  43.2 0.0 copy-done.3
  43.3 0.0 copy-done.4
  43.3 1.3 %finish.1 = (bf16[128,768]{1,0:T(8,128)(2,1)}, bf16[256,384]{1,0:T(8,128)(2,1)}, bf16[256,384]{1,0:T(8,128)(2,1)}, bf16[256,384]{1,0:T(8,128)(2,1)}, bf16[256,384]{1,0:T(8,128)(2,1)}) custom-call(bf16[256,384]{1,0:T(8,128)(2,1)S(1)} %get-tuple-element.7.att, bf16[128,768]{1,0:T(8,128)(2,1)S(1)} %get-tuple-element.8.rows, bf16[256,384]{1,0:T(8,128)(2,1)S(1)} %copy-done.2, ...), custom_call_target="tpu_custom_call" | custom-call | tf_op jit(solution)/shard_map/finish/pallas_call | solution.py:389
Async XLA Ops:
  0.6 1.4 %copy-start.5 = (s32[6,256]{1,0:T(8,128)S(1)}, s32[6,256]{1,0:T(8,128)}, u32[]{:S(2)}) copy-start(s32[6,256]{1,0:T(8,128)} %rank.1) | copy-start | bytes 18436
  1.3 0.7 %copy-start.6 = (s32[6,64]{1,0:T(8,128)S(1)}, s32[6,64]{1,0:T(8,128)}, u32[]{:S(2)}) copy-start(s32[6,64]{1,0:T(8,128)} %sizes.1) | copy-start | bytes 4612
  2.0 1.1 %copy-start = (bf16[3,256,384]{2,1,0:T(8,128)(2,1)S(1)}, bf16[3,256,384]{2,1,0:T(8,128)(2,1)}, u32[]{:S(2)}) copy-start(bf16[3,256,384]{2,1,0:T(8,128)(2,1)} %qkv.1) | copy-start | bytes 1769476
  3.1 0.9 %copy-start.1 = (bf16[256,384]{1,0:T(8,128)(2,1)S(1)}, bf16[256,384]{1,0:T(8,128)(2,1)}, u32[]{:S(2)}) copy-start(bf16[256,384]{1,0:T(8,128)(2,1)} %uncond.1) | copy-start | bytes 589828
  4.0 0.7 %copy-start.7 = (s32[6,64]{1,0:T(8,128)S(1)}, s32[6,64]{1,0:T(8,128)}, u32[]{:S(2)}) copy-start(s32[6,64]{1,0:T(8,128)} %owner.1) | copy-start | bytes 4612
  4.7 38.5 %copy-start.2 = (bf16[256,384]{1,0:T(8,128)(2,1)S(1)}, bf16[256,384]{1,0:T(8,128)(2,1)}, u32[]{:S(2)}) copy-start(bf16[256,384]{1,0:T(8,128)(2,1)} %zero.1) | copy-start | bytes 589828
  4.7 38.5 %copy-start.3 = (bf16[256,384]{1,0:T(8,128)(2,1)S(1)}, bf16[256,384]{1,0:T(8,128)(2,1)}, u32[]{:S(2)}) copy-start(bf16[256,384]{1,0:T(8,128)(2,1)} %one.1) | copy-start | bytes 589828
  4.7 38.5 %copy-start.4 = (bf16[256,384]{1,0:T(8,128)(2,1)S(1)}, bf16[256,384]{1,0:T(8,128)(2,1)}, u32[]{:S(2)}) copy-start(bf16[256,384]{1,0:T(8,128)(2,1)} %two.1) | copy-start | bytes 589828

commit v2 on v1

v2 whole, which is shorter than its diff:
```python
import functools
import math

import jax
import jax.numpy as jnp
from jax import lax
from jax.experimental import pallas as pl
from jax.experimental.pallas import tpu as pltpu
from jax.sharding import PartitionSpec as P

HEAD_DIM = 64
LANES = 128
STEP_GAP = 2
GUIDE = 6.0
EPS = 1e-05
F32 = jnp.float32
BF16 = jnp.bfloat16
MESH = pl.DeviceIdType.MESH
NEG = -1e30
SCORE_SCALE = math.log2(math.e) / math.sqrt(HEAD_DIM)


def mm(a, b):
    return jnp.dot(a, b, preferred_element_type=F32)


def mm_nt(a, b):
    return lax.dot_general(a, b, (((1,), (1,)), ((), ())), preferred_element_type=F32)


def iota(shape, axis):
    return lax.broadcasted_iota(jnp.int32, shape, axis)


def stride_of(groups):
    for step in range(max(groups // 2 - 1, 1), 0, -1):
        if math.gcd(step, groups) == 1:
            return step
    return 1


def loop(count, act):
    def body(k, c):
        act(k)
        return c

    lax.fori_loop(1, count, body, 0)


def exchange_kernel(
    groups,
    head_peers,
    qkv_hbm,
    rank_hbm,
    sizes_hbm,
    owner_hbm,
    uncond_hbm,
    att_hbm,
    rows_hbm,
    qkv,
    rank,
    sizes,
    owner,
    uncond,
    att_out,
    rows_out,
    send,
    recv,
    tag_send,
    tag_recv,
    back,
    home,
    gsend,
    grecv,
    codes,
    fetch,
    store,
    ts,
    tr,
    fs,
    fr,
    bs,
    br,
    hs,
    hr,
):
    me = lax.axis_index("tok")
    my_head = lax.axis_index("head")
    heads, toks = rank.shape
    pairs = heads // 2
    nclust = sizes.shape[1]
    half = back.shape[2]
    slots = 2 * half
    halves = groups * half
    total = groups * slots
    stride = stride_of(groups)

    fetches = [
        pltpu.make_async_copy(src, dst, fetch.at[i])
        for i, (src, dst) in enumerate(
            (
                (sizes_hbm, sizes),
                (owner_hbm, owner),
                (rank_hbm, rank),
                (qkv_hbm, qkv),
                (uncond_hbm, uncond),
            )
        )
    ]
    for one in fetches:
        one.start()

    barrier = pltpu.get_barrier_semaphore()

    def greet(axis, count, mine):
        loop(
            count,
            lambda k: pl.semaphore_signal(
                barrier,
                inc=1,
                device_id={axis: lax.rem(mine + k, count)},
                device_id_type=MESH,
            ),
        )

    greet("tok", groups, me)
    greet("head", head_peers, my_head)

    upto = jnp.where(iota((nclust, nclust), 1) <= iota((nclust, nclust), 0), 1.0, 0.0).astype(BF16)
    before = jnp.where(iota((nclust, nclust), 1) < iota((nclust, nclust), 0), 1.0, 0.0).astype(BF16)
    earlier_mat = jnp.where(iota((toks, toks), 0) < iota((toks, toks), 1), 1.0, 0.0).astype(BF16)
    group_iota = iota((groups, nclust), 0)
    group_base = iota((groups, toks), 0).astype(F32)

    fetches[0].wait()
    size_all = sizes[...]
    size_hi = (size_all >> 7).astype(F32).astype(BF16)
    size_lo = (size_all & 127).astype(F32).astype(BF16)
    ends = mm_nt(upto, size_hi) * 128.0 + mm_nt(upto, size_lo)
    starts = mm_nt(before, size_hi) * 128.0 + mm_nt(before, size_lo)
    fetches[1].wait()
    fetches[2].wait()

    hits = []
    insides = []
    owns = []
    for h in range(heads):
        ranks = rank[h : h + 1, :].astype(F32)
        passed = jnp.where(ends[:, h : h + 1] <= ranks, 1.0, 0.0)
        begun = jnp.where(starts[:, h : h + 1] <= ranks, 1.0, 0.0)
        insides.append((begun - passed).astype(BF16))
        owns.append(jnp.where(group_iota == owner[h : h + 1, :], 1.0, 0.0))
        hits.append(mm(owns[h].astype(BF16), insides[h]))
    all_hits = jnp.concatenate(hits, axis=0)
    earlier = mm(all_hits.astype(BF16), earlier_mat)
    counts = jnp.sum(all_hits, axis=1, keepdims=True)
    slot_rows = []
    spots = []
    codes[...] = jnp.full(codes.shape, -1.0, F32)
    for h in range(heads):
        lo = h * groups
        hit = hits[h]
        place = earlier[lo : lo + groups]
        if h % 2 == 1:
            place = place + counts[lo - groups : lo]
        spot = jnp.sum(hit * place, axis=0, keepdims=True)
        dest = jnp.sum(hit * group_base, axis=0, keepdims=True)
        spots.append(spot)
        slot_rows.append((dest * slots + spot).astype(jnp.int32))
        code = dest * half + spot
        codes[h : h + 1, :] = jnp.where(spot < half, code, -1.0)
        codes[heads + h : heads + h + 1, :] = jnp.where(spot >= half, code - half, -1.0)

    lane_tok = iota((toks, LANES), 1)
    lane_half = iota((halves, LANES), 1)
    slot_iota = iota((total, toks), 0)

    def pack(p):
        cols = slice(p * LANES, (p + 1) * LANES)
        q = qkv[0, :, cols].astype(F32)
        k = qkv[1, :, cols].astype(F32)
        v = qkv[2, :, cols].astype(F32)
        q_turn = pltpu.roll(q, HEAD_DIM, 1)
        k_turn = pltpu.roll(k, HEAD_DIM, 1)
        v_turn = pltpu.roll(v, HEAD_DIM, 1)
        low = lane_tok < HEAD_DIM
        sides = (
            (jnp.where(low, q, k_turn), jnp.where(low, v, v_turn)),
            (jnp.where(low, q_turn, k), jnp.where(low, v_turn, v)),
        )
        out = None
        for side in range(2):
            pick = jnp.where(slot_iota == slot_rows[2 * p + side], 1.0, 0.0).astype(BF16)
            part = mm(pick, jnp.concatenate(sides[side], axis=1).astype(BF16))
            out = part if out is None else out + part
        out = out.reshape(groups, slots, 2 * LANES)
        send[p, :, :slots] = out[:, :, :LANES].astype(BF16)
        v_low = out[:, :half, LANES:].reshape(halves, LANES)
        v_high = out[:, half:, LANES:].reshape(halves, LANES)
        v_both = jnp.where(lane_half < HEAD_DIM, v_low, v_high).astype(BF16)
        send[p, :, slots:] = v_both.reshape(groups, half, LANES)

    def pair_copy(src, dst, src_sem, dst_sem, p, to):
        return pltpu.make_async_remote_copy(
            src_ref=src.at[p, to],
            dst_ref=dst.at[p, me],
            send_sem=src_sem.at[p, to],
            recv_sem=dst_sem.at[p, me],
            device_id={"tok": to},
            device_id_type=MESH,
        )

    def pair_wait(src, dst, src_sem, dst_sem, p, at):
        return pltpu.make_async_remote_copy(
            src_ref=src.at[p, at],
            dst_ref=dst.at[p, at],
            send_sem=src_sem.at[p, at],
            recv_sem=dst_sem.at[p, at],
            device_id={"tok": at},
            device_id_type=MESH,
        )

    def other(k):
        return lax.rem(me + k * stride, groups)

    forward = (send, recv, fs, fr)
    backward = (back, home, bs, br)
    tagged = (tag_send, tag_recv, ts, tr)

    fetches[3].wait()
    for p in range(pairs):
        pack(p)
        if p == 0:
            pl.semaphore_wait(barrier, groups - 1 + head_peers - 1)
        loop(groups, lambda k: pair_copy(*forward, p, other(k)).start())
        recv[p, me] = send[p, me]
        if p == 0:
            lanes = tag_send.shape[3]
            tag_iota = iota((lanes, toks), 0).astype(F32)
            tags = None
            for h in range(heads):
                own = owns[h].astype(BF16)
                ordinal = mm_nt(own, before) + (1.0 + 128.0 * (h % 2))
                value = mm((owns[h] * ordinal).astype(BF16), insides[h]).astype(BF16)
                spread = tag_iota == spots[h] + float((h // 2) * slots)
                part = mm_nt(value, jnp.where(spread, 1.0, 0.0).astype(BF16))
                tags = part if tags is None else tags + part
            tag_send[0] = tags.reshape(groups, 1, lanes)
            loop(groups, lambda k: pair_copy(*tagged, 0, other(k)).start())
            tag_recv[0, me] = tag_send[0, me]

    code_cols = jnp.transpose(codes[...])
    back_iota = iota((toks, halves), 1).astype(F32)

    loop(groups, lambda k: pair_wait(*tagged, 0, other(k)).wait_recv())
    tag_lanes = tag_recv.shape[3]
    tags_in = tag_recv[0].reshape(groups, tag_lanes).astype(BF16)
    order = iota((total, groups), 0)
    source = jnp.where(order >= halves, order - halves, order) // half
    from_source = jnp.where(source == iota((total, groups), 1), 1.0, 0.0).astype(BF16)
    spread_tags = mm(from_source, tags_in)
    order = iota((total, tag_lanes), 0)
    spot_in = jnp.where(order >= halves, order - halves, order) % half + jnp.where(
        order >= halves, half, 0
    )
    tag_lane = iota((total, tag_lanes), 1)
    tag_rows = []
    tag_cols = []
    for p in range(pairs):
        kept = jnp.where(tag_lane == spot_in + p * slots, spread_tags, 0.0)
        tag_cols.append(jnp.sum(kept, axis=1, keepdims=True))
        tag_rows.append(mm_nt(jnp.ones((8, tag_lanes), BF16), kept.astype(BF16))[0:1, :])

    row_block = min(total, 256)
    for p in range(pairs):
        loop(groups, lambda k: pair_wait(*forward, p, other(k)).wait_recv())
        qk = jnp.concatenate(
            [
                recv[p, :, :half].reshape(halves, LANES),
                recv[p, :, half:slots].reshape(halves, LANES),
            ],
            axis=0,
        ).astype(F32)
        wide_lane = iota((total, LANES), 1)
        queries = jnp.where(wide_lane < HEAD_DIM, qk, 0.0).astype(BF16)
        keys = pltpu.roll(qk, HEAD_DIM, 1).astype(BF16)
        v_both = recv[p, :, slots:].reshape(halves, LANES).astype(F32)
        values = jnp.concatenate([v_both, pltpu.roll(v_both, HEAD_DIM, 1)], axis=0).astype(BF16)
        outs = []
        for i in range(total // row_block):
            here = slice(i * row_block, (i + 1) * row_block)
            scores = mm_nt(queries[here], keys)
            same = tag_cols[p][here] == tag_rows[p]
            masked = jnp.where(same, scores * SCORE_SCALE, NEG)
            largest = jnp.max(masked, axis=1, keepdims=True)
            expo = jnp.exp2(masked - largest)
            scale = 1.0 / jnp.sum(expo, axis=1, keepdims=True)
            outs.append(mm((expo * scale).astype(BF16), values))
        out = jnp.concatenate(outs, axis=0)
        packed = jnp.where(
            lane_half < HEAD_DIM, out[:halves], pltpu.roll(out[halves:], HEAD_DIM, 1)
        )
        back[p] = packed.astype(BF16).reshape(groups, half, LANES)
        loop(groups, lambda k: pair_copy(*backward, p, other(k)).start())
        home[p, me] = back[p, me]

    peer_rows = toks // head_peers

    def guide(p, k):
        dst = lax.rem(my_head + k, head_peers)
        return pltpu.make_async_remote_copy(
            src_ref=gsend.at[p, dst],
            dst_ref=grecv.at[p, my_head],
            send_sem=hs.at[p, dst],
            recv_sem=hr.at[p, my_head],
            device_id={"head": dst},
            device_id_type=MESH,
        )

    def guide_wait(p, k):
        src = lax.rem(my_head + k, head_peers)
        return pltpu.make_async_remote_copy(
            src_ref=gsend.at[p, src],
            dst_ref=grecv.at[p, src],
            send_sem=hs.at[p, src],
            recv_sem=hr.at[p, src],
            device_id={"head": src},
            device_id_type=MESH,
        )

    fetches[4].wait()
    for p in range(pairs):
        picks = []
        for h in (2 * p, 2 * p + 1):
            for row in (h, heads + h):
                hit = back_iota == code_cols[:, row : row + 1]
                picks.append(jnp.where(hit, 1.0, 0.0).astype(BF16))
        loop(groups, lambda k: pair_wait(*backward, p, other(k)).wait_recv())
        arrived = home[p].reshape(halves, LANES)
        a_low, a_high, b_low, b_high = [mm(pick, arrived) for pick in picks]
        left = a_low + pltpu.roll(a_high, HEAD_DIM, 1)
        right = b_high + pltpu.roll(b_low, HEAD_DIM, 1)
        att = jnp.where(lane_tok < HEAD_DIM, left, right)
        cols = slice(p * LANES, (p + 1) * LANES)
        att_out[:, cols] = att.astype(BF16)
        base = uncond[:, cols].astype(F32)
        guided = (base + GUIDE * (att - base)).astype(BF16)
        gsend[p] = guided.reshape(head_peers, peer_rows, LANES)
        loop(head_peers, lambda k: guide(p, k).start())
        grecv[p, my_head] = gsend[p, my_head]

    att_store = pltpu.make_async_copy(att_out, att_hbm, store.at[0])
    att_store.start()
    for p in range(pairs):
        loop(head_peers, lambda k: guide_wait(p, k).wait_recv())
        for src in range(head_peers):
            at = (src * pairs + p) * LANES
            rows_out[:, at : at + LANES] = grecv[p, src]
    rows_store = pltpu.make_async_copy(rows_out, rows_hbm, store.at[1])
    rows_store.start()

    loop(groups, lambda k: pair_wait(*tagged, 0, other(k)).wait_send())
    for p in range(pairs):
        loop(groups, lambda k: pair_wait(*forward, p, other(k)).wait_send())
        loop(groups, lambda k: pair_wait(*backward, p, other(k)).wait_send())
        loop(head_peers, lambda k: guide_wait(p, k).wait_send())
    att_store.wait()
    rows_store.wait()


def finish_kernel(
    att_hbm,
    rows_hbm,
    zero,
    one,
    two,
    gain,
    bias,
    normed,
    att_out,
    first_out,
    second_out,
    third_out,
    rows,
    fetch,
):
    att_fetch = pltpu.make_async_copy(att_hbm, att_out, fetch.at[0])
    rows_fetch = pltpu.make_async_copy(rows_hbm, rows, fetch.at[1])
    att_fetch.start()
    rows_fetch.start()
    att_fetch.wait()
    gap = 1.0 / STEP_GAP
    first = (att_out[...].astype(F32) - zero[...].astype(F32)) * gap
    first_out[...] = first.astype(BF16)
    second = (first - one[...].astype(F32)) * gap
    second_out[...] = second.astype(BF16)
    third = (second - two[...].astype(F32)) * gap
    third_out[...] = third.astype(BF16)
    rows_fetch.wait()
    guided = rows[...].astype(F32)
    inv = 1.0 / guided.shape[1]
    centered = guided - jnp.sum(guided, axis=1, keepdims=True) * inv
    var = jnp.sum(centered * centered, axis=1, keepdims=True) * inv
    normed[...] = (centered * lax.rsqrt(var + EPS) * gain[...].reshape(1, -1) + bias[...].reshape(1, -1)).astype(BF16)


def on_device(
    groups,
    head_peers,
    qkv,
    token_rank,
    cluster_sizes,
    cluster_owner,
    cache_zero,
    cache_one,
    cache_two,
    cache_uncond,
    norm_gain,
    norm_bias,
):
    heads, toks = token_rank.shape
    pairs = heads // 2
    width = norm_gain.shape[0]
    mine = cache_zero.shape[1]
    share = 2 * toks // groups
    slots = -(-share // 32) * 32
    half = slots // 2
    tag_lanes = -(-pairs * slots // LANES) * LANES
    peer_rows = toks // head_peers
    vmem = pl.BlockSpec(memory_space=pltpu.VMEM)
    hbm = pl.BlockSpec(memory_space=pltpu.HBM)
    att, rows = pl.pallas_call(
        functools.partial(exchange_kernel, groups, head_peers),
        out_shape=(
            jax.ShapeDtypeStruct((toks, mine), BF16),
            jax.ShapeDtypeStruct((peer_rows, width), BF16),
        ),
        in_specs=[hbm] * 5,
        out_specs=[hbm] * 2,
        scratch_shapes=[
            pltpu.VMEM(qkv.shape, BF16),
            pltpu.VMEM(token_rank.shape, jnp.int32),
            pltpu.VMEM(cluster_sizes.shape, jnp.int32),
            pltpu.VMEM(cluster_owner.shape, jnp.int32),
            pltpu.VMEM(cache_uncond.shape, BF16),
            pltpu.VMEM((toks, mine), BF16),
            pltpu.VMEM((peer_rows, width), BF16),
            pltpu.VMEM((pairs, groups, slots + half, LANES), BF16),
            pltpu.VMEM((pairs, groups, slots + half, LANES), BF16),
            pltpu.VMEM((1, groups, 1, tag_lanes), F32),
            pltpu.VMEM((1, groups, 1, tag_lanes), F32),
            pltpu.VMEM((pairs, groups, half, LANES), BF16),
            pltpu.VMEM((pairs, groups, half, LANES), BF16),
            pltpu.VMEM((pairs, head_peers, peer_rows, LANES), BF16),
            pltpu.VMEM((pairs, head_peers, peer_rows, LANES), BF16),
            pltpu.VMEM((LANES, toks), F32),
            pltpu.SemaphoreType.DMA((5,)),
            pltpu.SemaphoreType.DMA((2,)),
            pltpu.SemaphoreType.DMA((1, groups)),
            pltpu.SemaphoreType.DMA((1, groups)),
            pltpu.SemaphoreType.DMA((pairs, groups)),
            pltpu.SemaphoreType.DMA((pairs, groups)),
            pltpu.SemaphoreType.DMA((pairs, groups)),
            pltpu.SemaphoreType.DMA((pairs, groups)),
            pltpu.SemaphoreType.DMA((pairs, head_peers)),
            pltpu.SemaphoreType.DMA((pairs, head_peers)),
        ],
        compiler_params=pltpu.CompilerParams(
            collective_id=0, has_side_effects=True, vmem_limit_bytes=56 * 1024 * 1024
        ),
        name="exchange",
    )(qkv, token_rank, cluster_sizes, cluster_owner, cache_uncond)
    piece = jax.ShapeDtypeStruct((toks, mine), BF16)
    return pl.pallas_call(
        finish_kernel,
        out_shape=(jax.ShapeDtypeStruct((peer_rows, width), BF16), piece, piece, piece, piece),
        in_specs=[hbm] * 2 + [vmem] * 5,
        out_specs=[vmem] * 5,
        scratch_shapes=[
            pltpu.VMEM((peer_rows, width), BF16),
            pltpu.SemaphoreType.DMA((2,)),
        ],
        compiler_params=pltpu.CompilerParams(vmem_limit_bytes=56 * 1024 * 1024),
        name="finish",
    )(
        att,
        rows,
        cache_zero,
        cache_one,
        cache_two,
        norm_gain,
        norm_bias,
    )


def solution(mesh):
    sides = P("tok", "head")
    return jax.shard_map(
        functools.partial(on_device, mesh.shape["tok"], mesh.shape["head"]),
        mesh=mesh,
        in_specs=(
            P(None, "tok", "head"),
            P("head", "tok"),
            P("head", None),
            P("head", None),
            sides,
            sides,
            sides,
            sides,
            P(),
            P(),
        ),
        out_specs=(P(("tok", "head"), None), sides, sides, sides, sides),
        check_vma=False,
    )
```

time: 44.8 us -> 38.7 us (0.86)
  local copies, waits for them, and re-layouts: 4.09 us -> 0 us
  Pallas kernels: 39.8 us -> 37.9 us
    pallas_call x1, Pallas kernels: 38.5 us -> 34.7 us  [on_device(): pl.pallas_call(functools.partial(exchange_kernel, groups, head_peers), ou...]
    unnamed x16 -> x0, local copies, waits for them, and re-layouts: 2.69 us -> none
    pallas_call x1, Pallas kernels: 1.26 us -> 3.2 us  [on_device(): pl.pallas_call(finish_kernel, out_shape=(jax.ShapeDtypeStruct((peer_rows,...]
    reshape x2 -> x0, local copies, waits for them, and re-layouts: 1.4 us -> none  [the longest x1 0.7 us: on_device(): norm_bias.reshape(1, width)]
where the time goes in v2:
time: 38.7 us; the launch traced here: 38.5 us
  Pallas kernels  37.9 us (98%)
  between operations  0.64 us (2%)
    pallas_call x1, Pallas kernels, on_device(): pl.pallas_call(functools.partial(exchange_kernel, groups, head_peers), ou...  34.7 us
    pallas_call x1, Pallas kernels, on_device(): pl.pallas_call(finish_kernel, out_shape=(jax.ShapeDtypeStruct((peer_rows,...  3.2 us

profile of v2, /device:TPU:0, one launch (start us, length us, event | category | flops | bytes accessed | tf_op | source)
XLA Modules:
  0.0 38.5 jit_solution(1579887238071439427)
XLA Ops:
  0.6 34.7 %exchange.1 = (bf16[256,384]{1,0:T(8,128)(2,1)}, bf16[128,768]{1,0:T(8,128)(2,1)}) custom-call(bf16[3,256,384]{2,1,0:T(8,128)(2,1)} %qkv_hbm.1, s32[6,256]{1,0:T(8,128)} %rank_hbm.1, s32[6,64]{1,0:T(8,128)} %sizes_hbm.1, s32[6,64]{1,0:T(8,128)} %owner_hbm.1, bf16[256,384]{1,0:T(8,128)(2,1)} %uncond_hbm.1), custom_call_target="tpu_custom_call" | custom-call | tf_op jit(solution)/shard_map/exchange/pallas_call | solution.py:432
  35.3 3.2 %finish.1 = (bf16[128,768]{1,0:T(8,128)(2,1)}, bf16[256,384]{1,0:T(8,128)(2,1)}, bf16[256,384]{1,0:T(8,128)(2,1)}, bf16[256,384]{1,0:T(8,128)(2,1)}, bf16[256,384]{1,0:T(8,128)(2,1)}) custom-call(bf16[256,384]{1,0:T(8,128)(2,1)} %get-tuple-element.7.att_hbm, bf16[128,768]{1,0:T(8,128)(2,1)} %get-tuple-element.8.rows_hbm, bf16[256,384]{1,0:T(8,128)(2,1)} %zero.1, ...), custom_call_target="tpu_custom_call" | custom-call | tf_op jit(solution)/shard_map/finish/pallas_call | solution.py:474

commit v3 on v2

--- a/solution.py
+++ b/solution.py
@@ -44,7 +44,7 @@
         act(k)
         return c
 
-    lax.fori_loop(1, count, body, 0)
+    lax.fori_loop(1, count, body, 0, unroll=count <= 16)
 
 
 def exchange_kernel(
@@ -204,19 +204,20 @@
         return pltpu.make_async_remote_copy(
             src_ref=src.at[p, to],
             dst_ref=dst.at[p, me],
-            send_sem=src_sem.at[p, to],
-            recv_sem=dst_sem.at[p, me],
+            send_sem=src_sem.at[p],
+            recv_sem=dst_sem.at[p],
             device_id={"tok": to},
             device_id_type=MESH,
         )
 
-    def pair_wait(src, dst, src_sem, dst_sem, p, at):
+    def pair_wait(src, dst, src_sem, dst_sem, p):
+        rest = pl.ds(0, groups - 1)
         return pltpu.make_async_remote_copy(
-            src_ref=src.at[p, at],
-            dst_ref=dst.at[p, at],
-            send_sem=src_sem.at[p, at],
-            recv_sem=dst_sem.at[p, at],
-            device_id={"tok": at},
+            src_ref=src.at[p, rest],
+            dst_ref=dst.at[p, rest],
+            send_sem=src_sem.at[p],
+            recv_sem=dst_sem.at[p],
+            device_id={"tok": other(1)},
             device_id_type=MESH,
         )
 
@@ -252,7 +253,7 @@
     code_cols = jnp.transpose(codes[...])
     back_iota = iota((toks, halves), 1).astype(F32)
 
-    loop(groups, lambda k: pair_wait(*tagged, 0, other(k)).wait_recv())
+    pair_wait(*tagged, 0).wait_recv()
     tag_lanes = tag_recv.shape[3]
     tags_in = tag_recv[0].reshape(groups, tag_lanes).astype(BF16)
     order = iota((total, groups), 0)
@@ -273,7 +274,7 @@
 
     row_block = min(total, 256)
     for p in range(pairs):
-        loop(groups, lambda k: pair_wait(*forward, p, other(k)).wait_recv())
+        pair_wait(*forward, p).wait_recv()
         qk = jnp.concatenate(
             [
                 recv[p, :, :half].reshape(halves, LANES),
@@ -328,6 +329,9 @@
             device_id_type=MESH,
         )
 
+    pair_wait(*tagged, 0).wait_send()
+    for p in range(pairs):
+        pair_wait(*forward, p).wait_send()
     fetches[4].wait()
     for p in range(pairs):
         picks = []
@@ -335,7 +339,7 @@
             for row in (h, heads + h):
                 hit = back_iota == code_cols[:, row : row + 1]
                 picks.append(jnp.where(hit, 1.0, 0.0).astype(BF16))
-        loop(groups, lambda k: pair_wait(*backward, p, other(k)).wait_recv())
+        pair_wait(*backward, p).wait_recv()
         arrived = home[p].reshape(halves, LANES)
         a_low, a_high, b_low, b_high = [mm(pick, arrived) for pick in picks]
         left = a_low + pltpu.roll(a_high, HEAD_DIM, 1)
@@ -352,6 +356,8 @@
     att_store = pltpu.make_async_copy(att_out, att_hbm, store.at[0])
     att_store.start()
     for p in range(pairs):
+        pair_wait(*backward, p).wait_send()
+    for p in range(pairs):
         loop(head_peers, lambda k: guide_wait(p, k).wait_recv())
         for src in range(head_peers):
             at = (src * pairs + p) * LANES
@@ -359,10 +365,7 @@
     rows_store = pltpu.make_async_copy(rows_out, rows_hbm, store.at[1])
     rows_store.start()
 
-    loop(groups, lambda k: pair_wait(*tagged, 0, other(k)).wait_send())
-    for p in range(pairs):
-        loop(groups, lambda k: pair_wait(*forward, p, other(k)).wait_send())
-        loop(groups, lambda k: pair_wait(*backward, p, other(k)).wait_send())
+    for p in range(pairs):
         loop(head_peers, lambda k: guide_wait(p, k).wait_send())
     att_store.wait()
     rows_store.wait()
@@ -371,37 +374,71 @@
 def finish_kernel(
     att_hbm,
     rows_hbm,
+    zero_hbm,
+    one_hbm,
+    two_hbm,
+    gain_hbm,
+    bias_hbm,
+    normed_hbm,
+    att_out_hbm,
+    first_hbm,
+    second_hbm,
+    third_hbm,
+    att,
     zero,
     one,
     two,
+    rows,
     gain,
     bias,
-    normed,
-    att_out,
     first_out,
     second_out,
     third_out,
-    rows,
+    normed,
     fetch,
+    store,
 ):
-    att_fetch = pltpu.make_async_copy(att_hbm, att_out, fetch.at[0])
-    rows_fetch = pltpu.make_async_copy(rows_hbm, rows, fetch.at[1])
-    att_fetch.start()
-    rows_fetch.start()
-    att_fetch.wait()
+    sources = (att_hbm, zero_hbm, one_hbm, two_hbm, rows_hbm, gain_hbm, bias_hbm)
+    targets = (att, zero, one, two, rows, gain, bias)
+    fetches = [
+        pltpu.make_async_copy(src, dst, fetch.at[i])
+        for i, (src, dst) in enumerate(zip(sources, targets))
+    ]
+    for one_fetch in fetches:
+        one_fetch.start()
+    stores = []
+
+    def put(src, dst):
+        copy = pltpu.make_async_copy(src, dst, store.at[len(stores)])
+        copy.start()
+        stores.append(copy)
+
     gap = 1.0 / STEP_GAP
-    first = (att_out[...].astype(F32) - zero[...].astype(F32)) * gap
+    fetches[0].wait()
+    put(att, att_out_hbm)
+    fetches[1].wait()
+    first = (att[...].astype(F32) - zero[...].astype(F32)) * gap
     first_out[...] = first.astype(BF16)
+    put(first_out, first_hbm)
+    fetches[2].wait()
     second = (first - one[...].astype(F32)) * gap
     second_out[...] = second.astype(BF16)
+    put(second_out, second_hbm)
+    fetches[3].wait()
     third = (second - two[...].astype(F32)) * gap
     third_out[...] = third.astype(BF16)
-    rows_fetch.wait()
+    put(third_out, third_hbm)
+    for i in (4, 5, 6):
+        fetches[i].wait()
     guided = rows[...].astype(F32)
     inv = 1.0 / guided.shape[1]
     centered = guided - jnp.sum(guided, axis=1, keepdims=True) * inv
     var = jnp.sum(centered * centered, axis=1, keepdims=True) * inv
-    normed[...] = (centered * lax.rsqrt(var + EPS) * gain[...].reshape(1, -1) + bias[...].reshape(1, -1)).astype(BF16)
+    scaled = centered * lax.rsqrt(var + EPS) * gain[...].reshape(1, -1)
+    normed[...] = (scaled + bias[...].reshape(1, -1)).astype(BF16)
+    put(normed, normed_hbm)
+    for one_store in stores:
+        one_store.wait()
 
 
 def on_device(
@@ -427,7 +464,6 @@
     half = slots // 2
     tag_lanes = -(-pairs * slots // LANES) * LANES
     peer_rows = toks // head_peers
-    vmem = pl.BlockSpec(memory_space=pltpu.VMEM)
     hbm = pl.BlockSpec(memory_space=pltpu.HBM)
     att, rows = pl.pallas_call(
         functools.partial(exchange_kernel, groups, head_peers),
@@ -456,12 +492,12 @@
             pltpu.VMEM((LANES, toks), F32),
             pltpu.SemaphoreType.DMA((5,)),
             pltpu.SemaphoreType.DMA((2,)),
-            pltpu.SemaphoreType.DMA((1, groups)),
-            pltpu.SemaphoreType.DMA((1, groups)),
-            pltpu.SemaphoreType.DMA((pairs, groups)),
-            pltpu.SemaphoreType.DMA((pairs, groups)),
-            pltpu.SemaphoreType.DMA((pairs, groups)),
-            pltpu.SemaphoreType.DMA((pairs, groups)),
+            pltpu.SemaphoreType.DMA((1,)),
+            pltpu.SemaphoreType.DMA((1,)),
+            pltpu.SemaphoreType.DMA((pairs,)),
+            pltpu.SemaphoreType.DMA((pairs,)),
+            pltpu.SemaphoreType.DMA((pairs,)),
+            pltpu.SemaphoreType.DMA((pairs,)),
             pltpu.SemaphoreType.DMA((pairs, head_peers)),
             pltpu.SemaphoreType.DMA((pairs, head_peers)),
         ],
@@ -474,11 +510,17 @@
     return pl.pallas_call(
         finish_kernel,
         out_shape=(jax.ShapeDtypeStruct((peer_rows, width), BF16), piece, piece, piece, piece),
-        in_specs=[hbm] * 2 + [vmem] * 5,
-        out_specs=[vmem] * 5,
+        in_specs=[hbm] * 7,
+        out_specs=[hbm] * 5,
         scratch_shapes=[
+            *[pltpu.VMEM((toks, mine), BF16)] * 4,
             pltpu.VMEM((peer_rows, width), BF16),
-            pltpu.SemaphoreType.DMA((2,)),
+            pltpu.VMEM((width,), F32),
+            pltpu.VMEM((width,), F32),
+            *[pltpu.VMEM((toks, mine), BF16)] * 3,
+            pltpu.VMEM((peer_rows, width), BF16),
+            pltpu.SemaphoreType.DMA((7,)),
+            pltpu.SemaphoreType.DMA((5,)),
         ],
         compiler_params=pltpu.CompilerParams(vmem_limit_bytes=56 * 1024 * 1024),
         name="finish",

time: 38.7 us -> 36.2 us (0.935)
  Pallas kernels: 37.9 us -> 35.4 us
    pallas_call x1, Pallas kernels: 34.7 us -> 33.1 us  [on_device(): pl.pallas_call(functools.partial(exchange_kernel, groups, head_peers), ou...]
    pallas_call x1, Pallas kernels: 3.2 us -> 2.31 us  [on_device(): pl.pallas_call(finish_kernel, out_shape=(jax.ShapeDtypeStruct((peer_rows,...]
where the time goes in v3:
time: 36.2 us; the launch traced here: 36.1 us
  Pallas kernels  35.4 us (98%)
  between operations  0.64 us (2%)
    pallas_call x1, Pallas kernels, on_device(): pl.pallas_call(functools.partial(exchange_kernel, groups, head_peers), ou...  33.1 us
    pallas_call x1, Pallas kernels, on_device(): pl.pallas_call(finish_kernel, out_shape=(jax.ShapeDtypeStruct((peer_rows,...  2.31 us

profile of v3, /device:TPU:0, one launch (start us, length us, event | category | flops | bytes accessed | tf_op | source)
XLA Modules:
  0.0 36.1 jit_solution(10338740837649041072)
XLA Ops:
  0.6 33.1 %exchange.1 = (bf16[256,384]{1,0:T(8,128)(2,1)}, bf16[128,768]{1,0:T(8,128)(2,1)}) custom-call(bf16[3,256,384]{2,1,0:T(8,128)(2,1)} %qkv_hbm.1, s32[6,256]{1,0:T(8,128)} %rank_hbm.1, s32[6,64]{1,0:T(8,128)} %sizes_hbm.1, s32[6,64]{1,0:T(8,128)} %owner_hbm.1, bf16[256,384]{1,0:T(8,128)(2,1)} %uncond_hbm.1), custom_call_target="tpu_custom_call" | custom-call | tf_op jit(solution)/shard_map/exchange/pallas_call | solution.py:468
  33.8 2.3 %finish.1 = (bf16[128,768]{1,0:T(8,128)(2,1)}, bf16[256,384]{1,0:T(8,128)(2,1)}, bf16[256,384]{1,0:T(8,128)(2,1)}, bf16[256,384]{1,0:T(8,128)(2,1)}, bf16[256,384]{1,0:T(8,128)(2,1)}) custom-call(bf16[256,384]{1,0:T(8,128)(2,1)} %get-tuple-element.7.att_hbm, bf16[128,768]{1,0:T(8,128)(2,1)} %get-tuple-element.8.rows_hbm, bf16[256,384]{1,0:T(8,128)(2,1)} %zero_hbm.1, ...), custom_call_target="tpu_custom_call" | custom-call | tf_op jit(solution)/shard_map/finish/pallas_call | solution.py:510

commit v4 on v3

--- a/solution.py
+++ b/solution.py
@@ -63,7 +63,6 @@
     owner,
     uncond,
     att_out,
-    rows_out,
     send,
     recv,
     tag_send,
@@ -71,8 +70,8 @@
     back,
     home,
     gsend,
-    grecv,
     codes,
+    tag_cols,
     fetch,
     store,
     ts,
@@ -94,6 +93,9 @@
     halves = groups * half
     total = groups * slots
     stride = stride_of(groups)
+    chunk = tag_cols.shape[1] // slots
+    steps = groups // chunk
+    row_block = chunk * slots
 
     fetches = [
         pltpu.make_async_copy(src, dst, fetch.at[i])
@@ -256,23 +258,23 @@
     pair_wait(*tagged, 0).wait_recv()
     tag_lanes = tag_recv.shape[3]
     tags_in = tag_recv[0].reshape(groups, tag_lanes).astype(BF16)
-    order = iota((total, groups), 0)
-    source = jnp.where(order >= halves, order - halves, order) // half
-    from_source = jnp.where(source == iota((total, groups), 1), 1.0, 0.0).astype(BF16)
-    spread_tags = mm(from_source, tags_in)
-    order = iota((total, tag_lanes), 0)
-    spot_in = jnp.where(order >= halves, order - halves, order) % half + jnp.where(
-        order >= halves, half, 0
-    )
-    tag_lane = iota((total, tag_lanes), 1)
+    order = iota((total, 1), 0)
+    upper = order >= halves
+    inner = jnp.where(upper, order - halves, order)
+    lane_tags = iota((total, tag_lanes), 1)
+
+    def spread(source, spot, p):
+        from_source = jnp.where(source == iota((total, groups), 1), 1.0, 0.0).astype(BF16)
+        return jnp.where(lane_tags == spot + p * slots, mm(from_source, tags_in), 0.0)
+
     tag_rows = []
-    tag_cols = []
-    for p in range(pairs):
-        kept = jnp.where(tag_lane == spot_in + p * slots, spread_tags, 0.0)
-        tag_cols.append(jnp.sum(kept, axis=1, keepdims=True))
+    for p in range(pairs):
+        kept = spread(inner // half, inner % half + jnp.where(upper, half, 0), p)
         tag_rows.append(mm_nt(jnp.ones((8, tag_lanes), BF16), kept.astype(BF16))[0:1, :])
-
-    row_block = min(total, 256)
+        kept = spread(order // slots, order % slots, p)
+        column = jnp.sum(kept, axis=1, keepdims=True)
+        tag_cols[p * steps : (p + 1) * steps] = column.reshape(steps, row_block, 1)
+
     for p in range(pairs):
         pair_wait(*forward, p).wait_recv()
         qk = jnp.concatenate(
@@ -282,27 +284,42 @@
             ],
             axis=0,
         ).astype(F32)
-        wide_lane = iota((total, LANES), 1)
-        queries = jnp.where(wide_lane < HEAD_DIM, qk, 0.0).astype(BF16)
         keys = pltpu.roll(qk, HEAD_DIM, 1).astype(BF16)
         v_both = recv[p, :, slots:].reshape(halves, LANES).astype(F32)
         values = jnp.concatenate([v_both, pltpu.roll(v_both, HEAD_DIM, 1)], axis=0).astype(BF16)
-        outs = []
-        for i in range(total // row_block):
-            here = slice(i * row_block, (i + 1) * row_block)
-            scores = mm_nt(queries[here], keys)
-            same = tag_cols[p][here] == tag_rows[p]
+        lane_row = iota((row_block, LANES), 1)
+        lane_out = iota((chunk * half, LANES), 1)
+
+        def attend(i, c):
+            block = lax.rem(lax.div(me, chunk) + 1 + i, steps)
+            base = block * chunk
+            mine = recv[p, pl.ds(base, chunk), :slots].reshape(row_block, LANES).astype(F32)
+            queries = jnp.where(lane_row < HEAD_DIM, mine, 0.0).astype(BF16)
+            scores = mm_nt(queries, keys)
+            same = tag_cols[p * steps + block] == tag_rows[p]
             masked = jnp.where(same, scores * SCORE_SCALE, NEG)
             largest = jnp.max(masked, axis=1, keepdims=True)
             expo = jnp.exp2(masked - largest)
             scale = 1.0 / jnp.sum(expo, axis=1, keepdims=True)
-            outs.append(mm((expo * scale).astype(BF16), values))
-        out = jnp.concatenate(outs, axis=0)
-        packed = jnp.where(
-            lane_half < HEAD_DIM, out[:halves], pltpu.roll(out[halves:], HEAD_DIM, 1)
-        )
-        back[p] = packed.astype(BF16).reshape(groups, half, LANES)
-        loop(groups, lambda k: pair_copy(*backward, p, other(k)).start())
+            out = mm((expo * scale).astype(BF16), values).reshape(chunk, slots, LANES)
+            low = out[:, :half].reshape(chunk * half, LANES)
+            high = pltpu.roll(out[:, half:].reshape(chunk * half, LANES), HEAD_DIM, 1)
+            packed = jnp.where(lane_out < HEAD_DIM, low, high).astype(BF16)
+            back[p, pl.ds(base, chunk)] = packed.reshape(chunk, half, LANES)
+
+            def give(j, c):
+                to = base + lax.rem(me + j, chunk)
+
+                @pl.when(to != me)
+                def _():
+                    pair_copy(*backward, p, to).start()
+
+                return c
+
+            lax.fori_loop(0, chunk, give, 0, unroll=steps <= 2)
+            return c
+
+        lax.fori_loop(0, steps, attend, 0, unroll=steps <= 2)
         home[p, me] = back[p, me]
 
     peer_rows = toks // head_peers
@@ -311,7 +328,7 @@
         dst = lax.rem(my_head + k, head_peers)
         return pltpu.make_async_remote_copy(
             src_ref=gsend.at[p, dst],
-            dst_ref=grecv.at[p, my_head],
+            dst_ref=rows_hbm.at[my_head, p],
             send_sem=hs.at[p, dst],
             recv_sem=hr.at[p, my_head],
             device_id={"head": dst},
@@ -322,7 +339,7 @@
         src = lax.rem(my_head + k, head_peers)
         return pltpu.make_async_remote_copy(
             src_ref=gsend.at[p, src],
-            dst_ref=grecv.at[p, src],
+            dst_ref=rows_hbm.at[src, p],
             send_sem=hs.at[p, src],
             recv_sem=hr.at[p, src],
             device_id={"head": src},
@@ -333,6 +350,7 @@
     for p in range(pairs):
         pair_wait(*forward, p).wait_send()
     fetches[4].wait()
+    keeps = []
     for p in range(pairs):
         picks = []
         for h in (2 * p, 2 * p + 1):
@@ -351,7 +369,11 @@
         guided = (base + GUIDE * (att - base)).astype(BF16)
         gsend[p] = guided.reshape(head_peers, peer_rows, LANES)
         loop(head_peers, lambda k: guide(p, k).start())
-        grecv[p, my_head] = gsend[p, my_head]
+        keep = pltpu.make_async_copy(
+            gsend.at[p, my_head], rows_hbm.at[my_head, p], store.at[1 + p]
+        )
+        keep.start()
+        keeps.append(keep)
 
     att_store = pltpu.make_async_copy(att_out, att_hbm, store.at[0])
     att_store.start()
@@ -359,16 +381,11 @@
         pair_wait(*backward, p).wait_send()
     for p in range(pairs):
         loop(head_peers, lambda k: guide_wait(p, k).wait_recv())
-        for src in range(head_peers):
-            at = (src * pairs + p) * LANES
-            rows_out[:, at : at + LANES] = grecv[p, src]
-    rows_store = pltpu.make_async_copy(rows_out, rows_hbm, store.at[1])
-    rows_store.start()
-
     for p in range(pairs):
         loop(head_peers, lambda k: guide_wait(p, k).wait_send())
     att_store.wait()
-    rows_store.wait()
+    for keep in keeps:
+        keep.wait()
 
 
 def finish_kernel(
@@ -430,7 +447,8 @@
     put(third_out, third_hbm)
     for i in (4, 5, 6):
         fetches[i].wait()
-    guided = rows[...].astype(F32)
+    blocks = [rows[i, p] for i in range(rows.shape[0]) for p in range(rows.shape[1])]
+    guided = jnp.concatenate(blocks, axis=1).astype(F32)
     inv = 1.0 / guided.shape[1]
     centered = guided - jnp.sum(guided, axis=1, keepdims=True) * inv
     var = jnp.sum(centered * centered, axis=1, keepdims=True) * inv
@@ -462,6 +480,7 @@
     share = 2 * toks // groups
     slots = -(-share // 32) * 32
     half = slots // 2
+    chunk = math.gcd(groups, max(256 // slots, 1))
     tag_lanes = -(-pairs * slots // LANES) * LANES
     peer_rows = toks // head_peers
     hbm = pl.BlockSpec(memory_space=pltpu.HBM)
@@ -469,7 +488,7 @@
         functools.partial(exchange_kernel, groups, head_peers),
         out_shape=(
             jax.ShapeDtypeStruct((toks, mine), BF16),
-            jax.ShapeDtypeStruct((peer_rows, width), BF16),
+            jax.ShapeDtypeStruct((head_peers, pairs, peer_rows, LANES), BF16),
         ),
         in_specs=[hbm] * 5,
         out_specs=[hbm] * 2,
@@ -480,7 +499,6 @@
             pltpu.VMEM(cluster_owner.shape, jnp.int32),
             pltpu.VMEM(cache_uncond.shape, BF16),
             pltpu.VMEM((toks, mine), BF16),
-            pltpu.VMEM((peer_rows, width), BF16),
             pltpu.VMEM((pairs, groups, slots + half, LANES), BF16),
             pltpu.VMEM((pairs, groups, slots + half, LANES), BF16),
             pltpu.VMEM((1, groups, 1, tag_lanes), F32),
@@ -488,10 +506,10 @@
             pltpu.VMEM((pairs, groups, half, LANES), BF16),
             pltpu.VMEM((pairs, groups, half, LANES), BF16),
             pltpu.VMEM((pairs, head_peers, peer_rows, LANES), BF16),
-            pltpu.VMEM((pairs, head_peers, peer_rows, LANES), BF16),
             pltpu.VMEM((LANES, toks), F32),
+            pltpu.VMEM((pairs * groups // chunk, chunk * slots, 1), F32),
             pltpu.SemaphoreType.DMA((5,)),
-            pltpu.SemaphoreType.DMA((2,)),
+            pltpu.SemaphoreType.DMA((1 + pairs,)),
             pltpu.SemaphoreType.DMA((1,)),
             pltpu.SemaphoreType.DMA((1,)),
             pltpu.SemaphoreType.DMA((pairs,)),
@@ -514,7 +532,7 @@
         out_specs=[hbm] * 5,
         scratch_shapes=[
             *[pltpu.VMEM((toks, mine), BF16)] * 4,
-            pltpu.VMEM((peer_rows, width), BF16),
+            pltpu.VMEM((head_peers, pairs, peer_rows, LANES), BF16),
             pltpu.VMEM((width,), F32),
             pltpu.VMEM((width,), F32),
             *[pltpu.VMEM((toks, mine), BF16)] * 3,

time: 36.2 us -> 34.8 us (0.961)
  Pallas kernels: 35.4 us -> 34 us
    pallas_call x1, Pallas kernels: 33.1 us -> 31.7 us  [on_device(): pl.pallas_call(functools.partial(exchange_kernel, groups, head_peers), ou...]
where the time goes in v4:
time: 34.8 us; the launch traced here: 34.6 us
  Pallas kernels  34 us (98%)
  between operations  0.64 us (2%)
    pallas_call x1, Pallas kernels, on_device(): pl.pallas_call(functools.partial(exchange_kernel, groups, head_peers), ou...  31.7 us
    pallas_call x1, Pallas kernels, on_device(): pl.pallas_call(finish_kernel, out_shape=(jax.ShapeDtypeStruct((peer_rows,...  2.31 us

profile of v4, /device:TPU:0, one launch (start us, length us, event | category | flops | bytes accessed | tf_op | source)
XLA Modules:
  0.0 34.6 jit_solution(7611937491011806874)
XLA Ops:
  0.6 31.7 %exchange.1 = (bf16[256,384]{1,0:T(8,128)(2,1)}, bf16[2,3,128,128]{3,2,1,0:T(8,128)(2,1)}) custom-call(bf16[3,256,384]{2,1,0:T(8,128)(2,1)} %qkv_hbm.1, s32[6,256]{1,0:T(8,128)} %rank_hbm.1, s32[6,64]{1,0:T(8,128)} %sizes_hbm.1, s32[6,64]{1,0:T(8,128)} %owner_hbm.1, bf16[256,384]{1,0:T(8,128)(2,1)} %uncond_hbm.1), custom_call_target="tpu_custom_call" | custom-call | tf_op jit(solution)/shard_map/exchange/pallas_call | solution.py:487
  32.3 2.3 %finish.1 = (bf16[128,768]{1,0:T(8,128)(2,1)}, bf16[256,384]{1,0:T(8,128)(2,1)}, bf16[256,384]{1,0:T(8,128)(2,1)}, bf16[256,384]{1,0:T(8,128)(2,1)}, bf16[256,384]{1,0:T(8,128)(2,1)}) custom-call(bf16[256,384]{1,0:T(8,128)(2,1)} %get-tuple-element.7.att_hbm, bf16[2,3,128,128]{3,2,1,0:T(8,128)(2,1)} %get-tuple-element.8.rows_hbm, bf16[256,384]{1,0:T(8,128)(2,1)} %zero_hbm.1, ...), custom_call_target="tpu_custom_call" | custom-call | tf_op jit(solution)/shard_map/finish/pallas_call | solution.py:528
